TPU v7x, 128 devices: a whole 4x4x4 slice. The times are simulated.
128 devices in a mesh: frame: 16 (over z, y_hi, core), fsdp: 8 (over x, y_lo).
Axes of the slice: x: 4, y: 4 (y_hi: 2, y_lo: 2; y = y_hi * 2 + y_lo), z: 4, core: 2. Of those that a mesh axis runs over, the one named last changes fastest.
Arguments:
- hidden_states: bfloat16 [32, 512, 3072], P('frame', 'fsdp'), may hold values from -150 to 150, as said below
- teacher: bfloat16 [32, 512, 3072], P('frame', 'fsdp'), may hold values from -160 to 160
- mod_scale: float32 [3072], replicated, may hold values from -1.2 to 1.2
- mod_shift: float32 [3072], replicated, may hold values from -2 to 2
- out_gate: float32 [3072], replicated, may hold values from 0.5 to 1.5
- w_qkv: bfloat16 [3, 3072, 3072], P(None, None, 'fsdp'), may hold values from -0.109375 to 0.109375
- w_out: bfloat16 [3072, 3072], P('fsdp'), may hold values from -0.109375 to 0.109375
Outputs:
- grad_hidden: bfloat16 [32, 512, 3072], P('frame', 'fsdp')
- grad_w_qkv: bfloat16 [3, 3072, 3072], P(None, 'frame', 'fsdp')
- grad_w_out: bfloat16 [3072, 3072], P('fsdp', 'frame')
- grad_scale: float32 [3072], replicated
- grad_shift: float32 [3072], replicated
- grad_gate: float32 [3072], replicated
Inputs may be any that keep to these rules, and one draw needn't show every extreme that they name: `hidden_states`: each token and each feature carries a scale of its own.
All inputs are finite; a program needn't handle non-finite values.
Results may differ from a plain program's by a relative error of at most 0.018.
Values may be sent and summed in bfloat16 or wider, within the bound.
A program may use at most 192 MiB of HBM per device.

v0:
```python
import jax
import jax.numpy as jnp
from jax import lax
from jax.sharding import PartitionSpec as P

HEAD_DIM = 128


def head_norm(values):
    factor = lax.rsqrt(jnp.mean(values * values, -1, keepdims=True) + 1e-06)
    return (values * factor, factor)


def norm_back(grad_in, normed, factor):
    return factor * (grad_in - normed * jnp.mean(grad_in * normed, -1, keepdims=True))


def shards(hidden_states, teacher, mod_scale, mod_shift, out_gate, w_qkv, w_out):
    frames_dev, patch_dev, width = hidden_states.shape
    local_width = w_out.shape[0]
    heads_loc = local_width // HEAD_DIM
    inv_root = HEAD_DIM ** (-0.5)
    states = hidden_states.astype(jnp.float32)
    factor = lax.rsqrt(jnp.mean(states * states, -1, keepdims=True) + 1e-06)
    normed = states * factor
    modded = (normed * (1.0 + mod_scale) + mod_shift).astype(jnp.bfloat16)
    gathered = lax.all_gather(modded, "fsdp", axis=1, tiled=True)
    patches = gathered.shape[1]
    tok_count = frames_dev * patches
    flat = gathered.reshape(tok_count, width)
    proj = jnp.einsum("td,cdh->cth", flat, w_qkv, preferred_element_type=jnp.float32)
    q_norm, q_fac = head_norm(proj[0].reshape(tok_count, heads_loc, HEAD_DIM))
    k_norm, k_fac = head_norm(proj[1].reshape(tok_count, heads_loc, HEAD_DIM))
    packed = jnp.stack(
        [
            q_norm.astype(jnp.bfloat16).reshape(tok_count, local_width),
            k_norm.astype(jnp.bfloat16).reshape(tok_count, local_width),
            proj[2].astype(jnp.bfloat16),
        ],
        axis=1,
    ).reshape(frames_dev, patches, 3, local_width)
    pixels = lax.all_to_all(packed, "frame", split_axis=1, concat_axis=0, tiled=True)
    frames_all, pix_count = (pixels.shape[0], pixels.shape[1])
    split = pixels.reshape(frames_all, pix_count, 3, heads_loc, HEAD_DIM)
    queries, keys, values = (split[:, :, 0], split[:, :, 1], split[:, :, 2])
    scores = (
        jnp.einsum("fphe,gphe->phfg", queries, keys, preferred_element_type=jnp.float32) * inv_root
    )
    expo = jnp.exp(scores)
    probs = expo / jnp.sum(expo, -1, keepdims=True)
    probs_low = probs.astype(jnp.bfloat16)
    attended = jnp.einsum(
        "phfg,gphe->fphe", probs_low, values, preferred_element_type=jnp.float32
    ).astype(jnp.bfloat16)
    attended = attended.reshape(frames_all, pix_count, local_width)
    by_token = lax.all_to_all(attended, "frame", split_axis=0, concat_axis=1, tiled=True)
    block = by_token
    mixed = jnp.transpose(
        lax.psum_scatter(
            jnp.einsum("fph,hd->pfd", block, w_out, preferred_element_type=jnp.float32).astype(
                jnp.bfloat16
            ),
            "fsdp",
            scatter_dimension=0,
            tiled=True,
        ).astype(jnp.float32),
        (1, 0, 2),
    )
    diff = states + out_gate * mixed - teacher.astype(jnp.float32)
    upstream = (out_gate * diff).astype(jnp.bfloat16)
    up_all = lax.all_gather(upstream, "fsdp", axis=1, tiled=True)
    out_grad_local = jnp.einsum("fph,fpd->hd", by_token, up_all, preferred_element_type=jnp.float32)
    attn_grad = jnp.einsum("fpd,hd->fph", up_all, w_out, preferred_element_type=jnp.float32).astype(
        jnp.bfloat16
    )
    grad_pix = lax.all_to_all(attn_grad, "frame", split_axis=1, concat_axis=0, tiled=True)
    grad_pix = grad_pix.reshape(frames_all, pix_count, heads_loc, HEAD_DIM)
    dprob = jnp.einsum("fphe,gphe->phfg", grad_pix, values, preferred_element_type=jnp.float32)
    dval = jnp.einsum(
        "phfg,fphe->gphe", probs_low, grad_pix, preferred_element_type=jnp.float32
    ).astype(jnp.bfloat16)
    dscore = (probs * (dprob - jnp.sum(probs * dprob, -1, keepdims=True))).astype(jnp.bfloat16)
    dquery = (
        jnp.einsum("phfg,gphe->fphe", dscore, keys, preferred_element_type=jnp.float32) * inv_root
    ).astype(jnp.bfloat16)
    dkey = (
        jnp.einsum("phfg,fphe->gphe", dscore, queries, preferred_element_type=jnp.float32)
        * inv_root
    ).astype(jnp.bfloat16)
    stacked = jnp.stack([dquery, dkey, dval], axis=2).reshape(frames_all, pix_count, 3, local_width)
    returned = lax.all_to_all(stacked, "frame", split_axis=0, concat_axis=1, tiled=True).reshape(
        tok_count, 3, local_width
    )
    grad_q = norm_back(
        returned[:, 0].astype(jnp.float32).reshape(tok_count, heads_loc, HEAD_DIM), q_norm, q_fac
    )
    grad_k = norm_back(
        returned[:, 1].astype(jnp.float32).reshape(tok_count, heads_loc, HEAD_DIM), k_norm, k_fac
    )
    dproj = jnp.stack(
        [
            grad_q.astype(jnp.bfloat16).reshape(tok_count, local_width),
            grad_k.astype(jnp.bfloat16).reshape(tok_count, local_width),
            returned[:, 2],
        ],
        axis=0,
    )
    qkv_grad_local = jnp.einsum("td,cth->cdh", flat, dproj, preferred_element_type=jnp.float32)
    qkv_grad, out_grad = (
        lax.psum_scatter(
            qkv_grad_local.astype(jnp.bfloat16), "frame", scatter_dimension=1, tiled=True
        ).astype(jnp.float32),
        lax.psum_scatter(
            out_grad_local.astype(jnp.bfloat16), "frame", scatter_dimension=1, tiled=True
        ).astype(jnp.float32),
    )
    dproj_blocks = dproj.reshape(3, frames_dev, patches, local_width)
    block = dproj_blocks
    dmod = jnp.transpose(
        lax.psum_scatter(
            jnp.einsum("cfph,cdh->pfd", block, w_qkv, preferred_element_type=jnp.float32).astype(
                jnp.bfloat16
            ),
            "fsdp",
            scatter_dimension=0,
            tiled=True,
        ).astype(jnp.float32),
        (1, 0, 2),
    )
    sums = lax.psum(
        (jnp.sum(dmod * normed, (0, 1)), jnp.sum(dmod, (0, 1)), jnp.sum(diff * mixed, (0, 1))),
        ("frame", "fsdp"),
    )
    dnorm = dmod * (1.0 + mod_scale)
    grad_hidden = (
        diff + factor * (dnorm - normed * jnp.mean(dnorm * normed, -1, keepdims=True))
    ).astype(jnp.bfloat16)
    return (
        grad_hidden,
        qkv_grad.astype(jnp.bfloat16),
        out_grad.astype(jnp.bfloat16),
        sums[0],
        sums[1],
        sums[2],
    )


def solution(mesh):
    in_specs = (
        P("frame", "fsdp", None),
        P("frame", "fsdp", None),
        P(),
        P(),
        P(),
        P(None, None, "fsdp"),
        P("fsdp", None),
    )
    out_specs = (
        P("frame", "fsdp", None),
        P(None, "frame", "fsdp"),
        P("fsdp", "frame"),
        P(),
        P(),
        P(),
    )
    return jax.shard_map(shards, mesh=mesh, in_specs=in_specs, out_specs=out_specs, check_vma=False)
```

profile of v0, /device:TPU:1, one launch (start us, length us, event | category | flops | bytes accessed | tf_op | source)
XLA Modules:
  0.0 1011.0 jit_solution(16590212259665874428)
XLA Ops:
  11.9 132.3 %all-gather.3.cloned.1.call-done = bf16[2,512,3072]{2,1,0:T(8,128)(2,1)} async-done(((bf16[2,64,3072]{2,1,0:T(8,128)(2,1)}), bf16[2,512,3072]{2,1,0:T(8,128)(2,1)}) %all-gather.3.cloned.1.call-update) | async-done | bytes 6291472 | tf_op jit(solution)/shard_map/all_gather | solution.py:27
  144.2 11.5 %convolution_bitcast_fusion = f32[3,1024,384]{2,1,0:T(8,128)S(1)} fusion(bf16[1024,3072,1]{1,0,2:T(8,128)(2,1)} %bitcast.189, bf16[3,3072,384]{2,1,0:T(8,128)(2,1)} %param.12), kind=kOutput, calls=%fused_computation.29 | convolution fusion | flops 7247757312 | bytes 18087936 | tf_op jit(solution)/shard_map/td,cdh->cth/dot_general | solution.py:31
  164.6 3.7 copy.129
  171.4 3.7 copy.127
  178.1 3.4 mul.212
  184.4 3.4 mul.216
  187.9 4.5 multiply_convert_fusion.4
  192.3 4.8 pad_maximum_fusion
  197.1 8.7 copy.131
  205.8 38.9 %all_to_all.63 = bf16[2,512,3,384]{3,0,2,1:T(2,128)(2,1)S(1)} all-to-all(bf16[2,512,3,384]{3,0,2,1:T(2,128)(2,1)} %copy.131), channel_id=1, replica_groups=mesh['frame'=16,'fsdp'=8] {'frame'}, dimensions={1} | all-to-all | bytes 4718592 | tf_op jit(solution)/shard_map/all_to_all | solution.py:42
  246.8 7.0 reshape.212
  253.8 5.4 fusion.55
  259.2 4.7 fusion.46
  268.1 18.7 %all_to_all.64 = bf16[32,32,384]{2,1,0:T(8,128)(2,1)S(1)} all-to-all(bf16[32,32,384]{2,1,0:T(8,128)(2,1)} %reshape.213), channel_id=1, replica_groups=mesh['frame'=16,'fsdp'=8] {'frame'}, dimensions={0} | all-to-all | bytes 1572864 | tf_op jit(solution)/shard_map/all_to_all | solution.py:56
  287.8 5.4 convert_bitcast_fusion.1
  293.3 127.4 %reduce-scatter.7.cloned.1.call-done = bf16[64,2,3072]{2,0,1:T(8,128)(2,1)} async-done(((bf16[512,2,3072]{2,0,1:T(8,128)(2,1)}), bf16[64,2,3072]{2,0,1:T(8,128)(2,1)}) %reduce-scatter.7.cloned.1.call-update) | async-done | bytes 786448 | tf_op jit(solution)/shard_map/reduce_scatter | solution.py:59
  423.4 130.1 %all-gather.5.cloned.1.call-done = bf16[2,512,3072]{2,1,0:T(8,128)(2,1)} async-done(((bf16[2,64,3072]{2,1,0:T(8,128)(2,1)}), bf16[2,512,3072]{2,1,0:T(8,128)(2,1)}) %all-gather.5.cloned.1.call-update) | async-done | bytes 6291472 | tf_op jit(solution)/shard_map/all_gather | solution.py:71
  553.5 5.6 fusion.38
  559.9 21.6 %all_to_all.65 = bf16[2,512,384]{2,0,1:T(2,128)(2,1)S(1)} all-to-all(bf16[2,512,384]{2,0,1:T(2,128)(2,1)S(1)} %copy.140), channel_id=1, replica_groups=mesh['frame'=16,'fsdp'=8] {'frame'}, dimensions={1} | all-to-all | bytes 1572864 | tf_op jit(solution)/shard_map/all_to_all | solution.py:76
  583.2 3.2 multiply_reduce_fusion.2
  602.7 5.3 all-to-all-start.3
  613.0 26.5 %all-to-all-done.3 = bf16[32,32,3,384]{3,1,2,0:T(8,128)(2,1)} async-done(((bf16[32,32,3,384]{3,1,2,0:T(8,128)(2,1)}), bf16[32,32,3,384]{3,1,2,0:T(8,128)(2,1)}, u32[]{:S(2)}, u32[]{:S(2)}) %all-to-all-start.3) | async-done | bytes 2359328 | tf_op jit(solution)/shard_map/all_to_all | solution.py:91
  663.3 4.4 fusion.36
  668.8 12.2 %convert_bitcast_fusion = bf16[3,3072,384]{1,2,0:T(8,128)(2,1)} fusion(bf16[1024,3072,1]{1,0,2:T(8,128)(2,1)} %bitcast.190, bf16[1,1024,384]{2,1,0:T(8,128)(2,1)S(1)} %copy-done.14, bf16[1,1024,384]{2,1,0:T(8,128)(2,1)S(1)} %get-tuple-element.43, bf16[1,1024,384]{2,1,0:T(8,128)(2,1)S(1)} %get-tuple-element.42), kind=kOutput, calls=%fused_computation.3 | convolution fusion | flops 7253655552 | bytes 15728640 | tf_op jit(solution)/shard_map/td,cth->cdh/dot_general | solution.py:108
  681.1 14.8 %copy.167 = bf16[3,3072,384]{2,0,1:T(4,128)(2,1)} copy(bf16[3,3072,384]{1,2,0:T(8,128)(2,1)} %convert_bitcast_fusion) | data formatting | bytes 14155776
  695.9 7.8 copy.173
  705.2 13.2 %fusion.2 = bf16[512,2,3072]{2,0,1:T(8,128)(2,1)} fusion(bf16[3,3072,384]{2,1,0:T(8,128)(2,1)} %param.12, bf16[1,2,512,384]{3,2,0,1:T(8,128)(2,1)S(1)} %bitcast.184, bf16[1,2,512,384]{3,2,0,1:T(8,128)(2,1)S(1)} %bitcast.186, bf16[1,2,512,384]{3,2,0,1:T(8,128)(2,1)S(1)} %bitcast.185), kind=kOutput, calls=%fused_computation.4 | convolution fusion | flops 7253262336 | bytes 15728640 | tf_op jit(solution)/shard_map/cfph,cdh->pfd/dot_general | solution.py:121
  719.7 8.2 bitcast_convert_fusion.1
  727.9 66.4 %reduce-scatter.13.cloned.1.call-done = bf16[192,1152]{1,0:T(8,128)(2,1)} async-done(((bf16[3072,1152]{1,0:T(8,128)(2,1)}), bf16[192,1152]{1,0:T(8,128)(2,1)}) %reduce-scatter.13.cloned.1.call-update) | async-done | bytes 442384
  796.5 129.9 %reduce-scatter.9.cloned.1.call-done = bf16[64,2,3072]{2,0,1:T(8,128)(2,1)} async-done(((bf16[512,2,3072]{2,0,1:T(8,128)(2,1)}), bf16[64,2,3072]{2,0,1:T(8,128)(2,1)}) %reduce-scatter.9.cloned.1.call-update) | async-done | bytes 786448 | tf_op jit(solution)/shard_map/reduce_scatter | solution.py:120
  930.0 67.8 %all-reduce = (f32[3072]{0:T(1024)}, f32[3072]{0:T(1024)}, f32[3072]{0:T(1024)}) all-reduce(f32[3072]{0:T(1024)S(1)} %get-tuple-element.36, f32[3072]{0:T(1024)S(1)} %convert_reduce_fusion, f32[3072]{0:T(1024)S(1)} %get-tuple-element.38), channel_id=1, replica_groups=mesh['frame'=16,'fsdp'=8] {'frame','fsdp'}, use_global_device_ids=true, to_apply=%region_13.0 | all-reduce | flops 9216 | bytes 73728 | tf_op jit(solution)/shard_map/psum | solution.py:130
  997.8 3.4 fusion.26
  (113 shorter events, 92.4 us)
Async XLA Ops:
  7.2 280.6 %copy-start = (bf16[384,3072]{1,0:T(8,128)(2,1)S(1)}, bf16[384,3072]{1,0:T(8,128)(2,1)}, u32[]{:S(2)}) copy-start(bf16[384,3072]{1,0:T(8,128)(2,1)} %param.13) | copy-start | bytes 7077892
  7.2 137.0 %all-gather.3.cloned.1.call-start = ((), (), s32[]{:S(2)}) async-start(), calls=%async_computation.8 | async-start | bytes 7077888 | tf_op jit(solution)/shard_map/all_gather | solution.py:27
  11.8 408.9 %reduce-scatter.7.cloned.1.call-start = ((), (), s32[]{:S(2)}) async-start(), calls=%async_computation.9 | async-start | bytes 7077888 | tf_op jit(solution)/shard_map/reduce_scatter | solution.py:59
  155.7 3.6 copy-start.5
  259.2 4.7 copy-start.9
  286.9 0.9 copy-start.19
  293.2 127.5 %copy-start.3 = (bf16[2,64,3072]{2,1,0:T(8,128)(2,1)S(1)}, bf16[2,64,3072]{2,1,0:T(8,128)(2,1)}, u32[]{:S(2)}) copy-start(bf16[2,64,3072]{2,1,0:T(8,128)(2,1)} %param.7) | copy-start | bytes 2359300
  293.2 127.5 %copy-start.21 = (f32[3072]{0:T(1024)S(1)}, f32[3072]{0:T(1024)}, u32[]{:S(2)}) copy-start(f32[3072]{0:T(1024)} %param.11) | copy-start | bytes 36868
  293.2 260.3 %all-gather.5.cloned.1.call-start = ((), (), s32[]{:S(2)}) async-start(), calls=%async_computation.10 | async-start | bytes 7077888 | tf_op jit(solution)/shard_map/all_gather | solution.py:71
  581.5 1.8 copy-start.2
  583.2 3.2 copy-start.8
  588.1 1.2 copy-start.11
  589.3 1.7 copy-start.10
  593.9 3.2 copy-start.12
  602.7 5.6 copy-start.4
  602.7 36.8 %all-to-all-start.3 = ((bf16[32,32,3,384]{3,1,2,0:T(8,128)(2,1)}), bf16[32,32,3,384]{3,1,2,0:T(8,128)(2,1)}, u32[]{:S(2)}, u32[]{:S(2)}) async-start(bf16[32,32,3,384]{3,1,2,0:T(8,128)(2,1)} %copy.148), calls=%async_computation.4 | async-start | bytes 4718592 | tf_op jit(solution)/shard_map/all_to_all | solution.py:91
  608.0 186.3 %reduce-scatter.13.cloned.1.call-start = ((), (), s32[]{:S(2)}) async-start(), calls=%async_computation.13 | async-start | bytes 7520256
  663.3 5.6 copy-start.14
  667.7 0.9 copy-start.15
  667.7 1.1 copy-start.17
  703.6 1.1 copy-start.13
  703.6 1.4 copy-start.16
  703.6 1.6 copy-start.18
  703.7 222.8 %reduce-scatter.9.cloned.1.call-start = ((), (), s32[]{:S(2)}) async-start(), calls=%async_computation.11 | async-start | bytes 7077888 | tf_op jit(solution)/shard_map/reduce_scatter | solution.py:120
  718.4 1.2 copy-start.20
  718.5 285.3 %reduce-scatter.11.cloned.1.call-start = ((), (), s32[]{:S(2)}) async-start(), calls=%async_computation.12 | async-start | bytes 2506752 | tf_op jit(solution)/shard_map/reduce_scatter | solution.py:113
  727.9 199.9 %copy-start.6 = (bf16[2,64,3072]{2,1,0:T(8,128)(2,1)S(1)}, bf16[2,64,3072]{2,1,0:T(8,128)(2,1)}, u32[]{:S(2)}) copy-start(bf16[2,64,3072]{2,1,0:T(8,128)(2,1)} %param.8) | copy-start | bytes 2359300
  727.9 199.9 %copy-start.7 = (bf16[64,2,3072]{2,0,1:T(8,128)(2,1)S(1)}, bf16[64,2,3072]{2,0,1:T(8,128)(2,1)}, u32[]{:S(2)}) copy-start(bf16[64,2,3072]{2,0,1:T(8,128)(2,1)} %reduce-scatter.7.cloned.1.call-done) | copy-start | bytes 2359300
  997.8 6.0 copy-start.1
Sparse Core Ops, SparseCore 0:
  11.9 132.2 all-gather.2
  293.3 127.3 reduce-scatter.6
  423.5 129.9 all-gather.4
  703.8 90.4 reduce-scatter.12
  796.7 129.7 reduce-scatter.8
  931.5 72.2 reduce-scatter.10
where the time goes:
time: 1020 us; the launch traced here: 1010 us
  waiting for transfers between devices  615 us (60%)
  blocking collectives  147 us (14%)
  local copies, waits for them, and re-layouts  117 us (11%)
  matrix products  70.4 us (7%)
  other arithmetic  40 us (4%)
  between operations  14.8 us (1%)
    all_gather x1, waiting for transfers between devices, shards(): gathered = lax.all_gather(modded, 'fsdp', axis=1, tiled=True)  132 us
    all_gather x1, waiting for transfers between devices, shards(): up_all = lax.all_gather(upstream, 'fsdp', axis=1, tiled=True)  130 us
    reduce_scatter x1, waiting for transfers between devices, shards(): lax.psum_scatter(jnp.einsum('cfph,cdh->pfd', block, w_qkv, preferred_elem...  130 us
    reduce_scatter x1, waiting for transfers between devices, shards(): lax.psum_scatter(jnp.einsum('fph,hd->pfd', block, w_out, preferred_elemen...  127 us
    psum x1, blocking collectives, shards(): lax.psum((jnp.sum(dmod * normed, (0, 1)), jnp.sum(dmod, (0, 1)), jnp.sum(...  67.8 us
    unnamed x7, waiting for transfers between devices  66.5 us
    all_to_all x1, blocking collectives, shards(): lax.all_to_all(packed, 'frame', split_axis=1, concat_axis=0, tiled=True)  38.9 us
    unnamed x48, local copies, waits for them, and re-layouts  30.6 us
  transfers between devices with their start and end apart: 7, of which 7 were waited for; matrix products, arithmetic and copies ran while one was open for 3% of the time, Pallas kernels for 0%

commit v1 on v0

v1 whole, which is shorter than its diff:
```python
import functools
import jax
import jax.numpy as jnp
from jax import lax
from jax.experimental import pallas as pl
from jax.experimental.pallas import tpu as pltpu
from jax.sharding import PartitionSpec as P

HEAD_DIM = 128
HEADS = 3
LOCAL = 384
WIDTH = 3072
HALF = 64
TILE = 512
INV_ROOT = HEAD_DIM ** (-0.5)
MESH = pl.DeviceIdType.MESH
BF = jnp.bfloat16
F32 = jnp.float32
VMEM_BYTES = 60 * 1024 * 1024


class Place:
    def __init__(self):
        fr = lax.axis_index("frame")
        fs = lax.axis_index("fsdp")
        self.fr = fr
        self.fs = fs
        self.x = lax.div(fs, 2)
        self.lo = lax.rem(fs, 2)
        self.core = lax.rem(fr, 2)
        self.group = lax.div(fr, 2)
        other = fs + 1 - 2 * self.lo
        hi = lax.rem(self.group, 2)
        self.right = (fr, lax.rem(fs + 2, 8))
        self.left = (fr, lax.rem(fs + 6, 8))
        self.side = ((fr, other), (fr + 2 - 4 * hi, other))

    def along(self, off):
        return lax.rem(self.x + off, 4)

    def meet(self):
        barrier = pltpu.get_barrier_semaphore()
        for peer in (self.right, self.left) + self.side:
            pl.semaphore_signal(barrier, inc=1, device_id=peer, device_id_type=MESH)

        def greet(step, carry):
            pl.semaphore_signal(
                barrier,
                inc=1,
                device_id=(lax.rem(self.fr + step, 16), self.fs),
                device_id_type=MESH,
            )
            return carry

        lax.fori_loop(1, 16, greet, 0)
        pl.semaphore_wait(barrier, 19)


def remote(src, dst, send_sem, recv_sem, device):
    return pltpu.make_async_remote_copy(
        src_ref=src,
        dst_ref=dst,
        send_sem=send_sem,
        recv_sem=recv_sem,
        device_id=device,
        device_id_type=MESH,
    )


def landed(ref, sem):
    pltpu.make_async_copy(ref, ref, sem).wait()


def loop(count, body):
    def step(i, carry):
        body(i)
        return carry

    lax.fori_loop(0, count, step, 0)


def near_first(p):
    return 3 * p - lax.div(5 * p * (p - 1), 2) + lax.div(4 * p * (p - 1) * (p - 2), 3)


def far_first(p):
    return 2 - p + lax.div(3 * p * (p - 1), 2) - lax.div(4 * p * (p - 1) * (p - 2), 3)


def gather_kernel(project, own, w_hbm, *refs):
    if project:
        full, sent_to, factors, weight, out, x_send, y_send, recv, o_send, o_recv, w_sem = refs
    else:
        full, sent_to, weight, out, x_send, y_send, recv, o_send, o_recv, w_sem = refs
    at = Place()
    if project:
        w_copies = [
            pltpu.make_async_copy(
                w_hbm.at[c], weight.at[:, pl.ds(c * LOCAL, LOCAL)], w_sem.at[c]
            )
            for c in range(3)
        ]
    else:
        w_copies = [pltpu.make_async_copy(w_hbm, weight, w_sem.at[0])]
    for copy in w_copies:
        copy.start()
    at.meet()

    def to_right(src, xi, h, n):
        return remote(src, full.at[0, xi, h], x_send.at[n], recv.at[0, xi, h], at.right)

    def to_left(src, xi, h, n):
        return remote(src, full.at[0, xi, h], x_send.at[n], recv.at[0, xi, h], at.left)

    def to_side(src, xi, h, n):
        return remote(src, full.at[1, xi, h], y_send.at[n], recv.at[1, xi, h], at.side[h])

    xl, xr, xf = at.along(3), at.along(1), at.along(2)
    first = [
        to_right(own.at[0], at.x, 0, 0),
        to_left(own.at[1], at.x, 1, 1),
        to_side(own.at[0], at.x, 0, 0),
        to_side(own.at[1], at.x, 1, 1),
        to_right(own.at[1], at.x, 1, 2),
        to_left(own.at[0], at.x, 0, 3),
    ]
    for copy in first:
        copy.start()
    full[0, at.x] = own[...]
    fwd = [
        to_right(full.at[0, xl, 0], xl, 0, 4),
        to_left(full.at[0, xr, 1], xr, 1, 5),
        to_side(full.at[0, xl, 0], xl, 0, 2),
        to_side(full.at[0, xl, 1], xl, 1, 3),
        to_side(full.at[0, xr, 0], xr, 0, 4),
        to_side(full.at[0, xr, 1], xr, 1, 5),
        to_side(full.at[0, xf, 0], xf, 0, 6),
        to_side(full.at[0, xf, 1], xf, 1, 7),
    ]
    for copy in w_copies:
        copy.wait()

    def arrived(slot, xi, h):
        landed(full.at[slot, xi, h], recv.at[slot, xi, h])

    def step(k):
        slot = lax.div(k, 4)
        xi = at.along(near_first(lax.rem(k, 4)))

        @pl.when(k == 1)
        def _():
            arrived(0, xl, 0)
            fwd[0].start()
            fwd[2].start()
            arrived(0, xr, 1)
            fwd[1].start()
            fwd[5].start()
            arrived(0, xl, 1)
            fwd[3].start()

        @pl.when(k == 2)
        def _():
            arrived(0, xr, 0)
            fwd[4].start()

        @pl.when(k == 3)
        def _():
            arrived(0, xf, 0)
            fwd[6].start()
            arrived(0, xf, 1)
            fwd[7].start()

        @pl.when(k >= 4)
        def _():
            arrived(1, xi, 0)
            arrived(1, xi, 1)

        tokens = full[slot, xi].reshape(2 * HALF, WIDTH)
        if project:
            both = jnp.dot(tokens, weight[...], preferred_element_type=F32)
            lane = lax.broadcasted_iota(jnp.int32, (2 * HALF, HEAD_DIM), 1)
            kept = jnp.zeros((2 * HALF, HEAD_DIM), F32)
            for j in range(3 * HEADS):
                block = both[:, j * HEAD_DIM : (j + 1) * HEAD_DIM]
                if j < 2 * HEADS:
                    factor = lax.rsqrt(jnp.mean(block * block, -1, keepdims=True) + 1e-06)
                    kept = jnp.where(lane == j, factor, kept)
                    block = block * factor
                out[k, :, :, j * HEAD_DIM : (j + 1) * HEAD_DIM] = block.astype(BF).reshape(
                    8, 16, HEAD_DIM
                )
            factors[slot, xi] = kept
        else:
            both = lax.dot_general(
                tokens, weight[...], (((1,), (1,)), ((), ())), preferred_element_type=F32
            )
            out[k] = both.astype(BF).reshape(8, 16, LOCAL)
        to_core = lax.rem(xi, 2)
        to_slot = 2 * lax.div(xi, 2) + lax.rem(at.lo + slot, 2)

        def give(g):
            target = 2 * g + to_core
            src = out.at[k, g]
            dst = sent_to.at[to_slot, at.fr]

            @pl.when(target == at.fr)
            def _():
                pltpu.make_async_copy(src, dst, o_recv.at[to_slot]).start()

            @pl.when(target != at.fr)
            def _():
                remote(src, dst, o_send.at[g], o_recv.at[to_slot], (target, at.fs)).start()

        loop(8, give)

    loop(8, step)

    for copy in first + fwd:
        copy.wait_send()

    def drain(g):
        @pl.when(g == at.group)
        def _():
            landed(out.at[pl.ds(0, 4), g], o_send.at[g])

        @pl.when(g != at.group)
        def _():
            landed(out.at[:, g], o_send.at[g])

    loop(8, drain)
    loop(4, lambda t: landed(sent_to.at[t], o_recv.at[t]))


def vmem(count):
    return [pl.BlockSpec(memory_space=pltpu.VMEM)] * count


def gather(own, weight, project):
    cols = 3 * LOCAL if project else LOCAL
    shapes = [
        jax.ShapeDtypeStruct((2, 4, 2, HALF, WIDTH), BF),
        jax.ShapeDtypeStruct((4, 16, 16, cols), BF),
    ]
    if project:
        shapes.append(jax.ShapeDtypeStruct((2, 4, 2 * HALF, HEAD_DIM), F32))
    flops = 2 * 1024 * WIDTH * cols
    return pl.pallas_call(
        functools.partial(gather_kernel, project),
        out_shape=shapes,
        in_specs=[pl.BlockSpec(memory_space=pltpu.VMEM), pl.BlockSpec(memory_space=pl.ANY)],
        out_specs=vmem(len(shapes)),
        scratch_shapes=[
            pltpu.VMEM((WIDTH, cols) if project else (LOCAL, WIDTH), BF),
            pltpu.VMEM((8, 8, 16, cols), BF),
            pltpu.SemaphoreType.DMA((6,)),
            pltpu.SemaphoreType.DMA((8,)),
            pltpu.SemaphoreType.DMA((2, 4, 2)),
            pltpu.SemaphoreType.DMA((8,)),
            pltpu.SemaphoreType.DMA((4,)),
            pltpu.SemaphoreType.DMA((3,)),
        ],
        compiler_params=pltpu.CompilerParams(
            collective_id=0 if project else 2,
            has_side_effects=True,
            vmem_limit_bytes=VMEM_BYTES,
        ),
        cost_estimate=pl.CostEstimate(flops=flops, bytes_accessed=30_000_000, transcendentals=0),
        name="gather_project" if project else "gather_back",
    )(own, weight)


def same_patch():
    rows = lax.broadcasted_iota(jnp.int32, (256, 256), 0)
    cols = lax.broadcasted_iota(jnp.int32, (256, 256), 1)
    return lax.rem(rows, 8) == lax.rem(cols, 8)


def dot_nt(a, b):
    return lax.dot_general(a, b, (((1,), (1,)), ((), ())), preferred_element_type=F32)


def dot_tn(a, b):
    return lax.dot_general(a, b, (((0,), (0,)), ((), ())), preferred_element_type=F32)


def softmax(query, key):
    scores = dot_nt(query, key) * INV_ROOT
    expo = jnp.where(same_patch(), jnp.exp(scores), 0.0)
    return expo / jnp.sum(expo, -1, keepdims=True)


def scatter_kernel(back, *refs):
    if back:
        qkv, grad, factors, w_hbm, total, tokens, dproj = refs[:7]
        refs = refs[7:]
    else:
        qkv, w_hbm, total, tokens = refs[:4]
        refs = refs[4:]
    (
        weight, out, part, mine, from_side, far, near,
        o_send, o_recv, y_send, y_recv, f_send, f_recv, n_send, n_recv, w_sem,
    ) = refs
    at = Place()
    if back:
        w_copies = [
            pltpu.make_async_copy(
                w_hbm.at[c], weight.at[:, pl.ds(c * LOCAL, LOCAL)], w_sem.at[c]
            )
            for c in range(3)
        ]
    else:
        w_copies = [pltpu.make_async_copy(w_hbm, weight, w_sem.at[0])]
    for copy in w_copies:
        copy.start()
    at.meet()

    def columns(ref, t, block):
        return ref[t, :, :, block * HEAD_DIM : (block + 1) * HEAD_DIM].reshape(256, HEAD_DIM)

    def put(i, block, value):
        out[i, :, :, block * HEAD_DIM : (block + 1) * HEAD_DIM] = value.astype(BF).reshape(
            16, 16, HEAD_DIM
        )

    def attend(i):
        slot = 1 - lax.div(i, 2)
        xh = lax.rem(i, 2)
        t = 2 * xh + lax.rem(at.lo + slot, 2)
        for h in range(HEADS):
            query, key, value = (columns(qkv, t, c * HEADS + h) for c in range(3))
            probs = softmax(query, key)
            low = probs.astype(BF)
            if not back:
                put(i, h, jnp.dot(low, value, preferred_element_type=F32))
                continue
            grad_in = columns(grad, t, h)
            dprob = dot_nt(grad_in, value)
            put(i, 2 * HEADS + h, dot_tn(low, grad_in))
            dscore = (probs * (dprob - jnp.sum(probs * dprob, -1, keepdims=True))).astype(BF)
            for c, normed, product in (
                (0, query, jnp.dot(dscore, key, preferred_element_type=F32)),
                (1, key, dot_tn(dscore, query)),
            ):
                step_in = (product * INV_ROOT).astype(BF).astype(F32)
                wide = normed.astype(F32)
                put(
                    i,
                    c * HEADS + h,
                    step_in - wide * jnp.mean(step_in * wide, -1, keepdims=True),
                )
        xi = 2 * xh + at.core

        def give(f):
            src = out.at[i, f]
            dst = tokens.at[slot, xi, at.group]

            @pl.when(f == at.fr)
            def _():
                pltpu.make_async_copy(src, dst, o_recv.at[slot, xi]).start()

            @pl.when(f != at.fr)
            def _():
                remote(src, dst, o_send.at[i], o_recv.at[slot, xi], (f, at.fs)).start()

        loop(16, give)

    loop(4, attend)
    for copy in w_copies:
        copy.wait()

    def product(slot, xi, j):
        tile = pl.ds(pl.multiple_of(j * TILE, TILE), TILE)
        if back:
            return tile, dot_nt(dproj[slot, xi], weight[tile, :])
        rows = tokens[slot, xi].reshape(2 * HALF, LOCAL)
        return tile, jnp.dot(rows, weight[:, tile], preferred_element_type=F32)

    def take(slot, xi):
        landed(tokens.at[slot, xi], o_recv.at[slot, xi])
        if back:
            for j in range(3 * HEADS):
                cols = slice(j * HEAD_DIM, (j + 1) * HEAD_DIM)
                block = tokens[slot, xi, :, :, cols].reshape(2 * HALF, HEAD_DIM)
                if j < 2 * HEADS:
                    block = (block.astype(F32) * factors[slot, xi, :, j : j + 1]).astype(BF)
                dproj[slot, xi, :, cols] = block

    def first(n):
        xi = at.along(far_first(n))
        take(1, xi)

        def tiles(j):
            tile, value = product(1, xi, j)
            part[xi, :, :, tile] = value.astype(BF).reshape(2, HALF, TILE)

        loop(WIDTH // TILE, tiles)
        for h in range(2):
            remote(
                part.at[xi, h], from_side.at[xi, h], y_send.at[xi, h], y_recv.at[xi, h], at.side[h]
            ).start()

    loop(4, first)

    xl, xr, xf = at.along(3), at.along(1), at.along(2)
    far_copies = [
        remote(mine.at[xf, 0], far.at[0], f_send.at[0], f_recv.at[0], at.right),
        remote(mine.at[xf, 1], far.at[1], f_send.at[1], f_recv.at[1], at.left),
    ]
    near_copies = [
        remote(mine.at[xr, 1], near.at[0, 1], n_send.at[0, 1], n_recv.at[0, 1], at.right),
        remote(mine.at[xl, 0], near.at[1, 0], n_send.at[1, 0], n_recv.at[1, 0], at.left),
        remote(mine.at[xr, 0], near.at[0, 0], n_send.at[0, 0], n_recv.at[0, 0], at.right),
        remote(mine.at[xl, 1], near.at[1, 1], n_send.at[1, 1], n_recv.at[1, 1], at.left),
    ]

    def second(n):
        xi = at.along(far_first(n))
        take(0, xi)
        for h in range(2):
            landed(from_side.at[xi, h], y_recv.at[xi, h])

        def tiles(j):
            tile, value = product(0, xi, j)
            other = from_side[xi, :, :, tile].astype(F32).reshape(2 * HALF, TILE)
            mine[xi, :, :, tile] = (value + other).astype(BF).reshape(2, HALF, TILE)

        loop(WIDTH // TILE, tiles)

        @pl.when(n == 0)
        def _():
            far_copies[0].start()
            far_copies[1].start()

        @pl.when(n == 1)
        def _():
            near_copies[0].start()

        @pl.when(n == 2)
        def _():
            near_copies[1].start()

    loop(4, second)
    for d, xi in ((0, xr), (1, xl)):
        landed(far.at[d], f_recv.at[d])

        def tiles(j, d=d, xi=xi):
            tile = pl.ds(pl.multiple_of(j * TILE, TILE), TILE)
            mine[xi, d, :, tile] = (
                mine[xi, d, :, tile].astype(F32) + far[d, :, tile].astype(F32)
            ).astype(BF)

        loop(WIDTH // TILE, tiles)
        near_copies[2 + d].start()
    for d, h in ((0, 1), (1, 0), (0, 0), (1, 1)):
        landed(near.at[d, h], n_recv.at[d, h])

    def finish(j):
        tile = pl.ds(pl.multiple_of(j * TILE, TILE), TILE)
        for h in range(2):
            total[h * HALF : (h + 1) * HALF, tile] = (
                mine[at.x, h, :, tile].astype(F32)
                + near[0, h, :, tile].astype(F32)
                + near[1, h, :, tile].astype(F32)
            )

    loop(WIDTH // TILE, finish)
    for copy in far_copies + near_copies:
        copy.wait_send()
    for xi in range(4):
        for h in range(2):
            landed(part.at[xi, h], y_send.at[xi, h])

    loop(4, lambda i: landed(out.at[i, pl.ds(0, 15)], o_send.at[i]))


def scatter(args, weight, back):
    cols = 3 * LOCAL if back else LOCAL
    shapes = [
        jax.ShapeDtypeStruct((2 * HALF, WIDTH), F32),
        jax.ShapeDtypeStruct((2, 4, 8, 16, cols), BF),
    ]
    if back:
        shapes.append(jax.ShapeDtypeStruct((2, 4, 2 * HALF, cols), BF))
    return pl.pallas_call(
        functools.partial(scatter_kernel, back),
        out_shape=shapes,
        in_specs=vmem(len(args)) + [pl.BlockSpec(memory_space=pl.ANY)],
        out_specs=vmem(len(shapes)),
        scratch_shapes=[
            pltpu.VMEM((WIDTH, cols) if back else (LOCAL, WIDTH), BF),
            pltpu.VMEM((4, 16, 16, cols), BF),
            pltpu.VMEM((4, 2, HALF, WIDTH), BF),
            pltpu.VMEM((4, 2, HALF, WIDTH), BF),
            pltpu.VMEM((4, 2, HALF, WIDTH), BF),
            pltpu.VMEM((2, HALF, WIDTH), BF),
            pltpu.VMEM((2, 2, HALF, WIDTH), BF),
            pltpu.SemaphoreType.DMA((4,)),
            pltpu.SemaphoreType.DMA((2, 4)),
            pltpu.SemaphoreType.DMA((4, 2)),
            pltpu.SemaphoreType.DMA((4, 2)),
            pltpu.SemaphoreType.DMA((2,)),
            pltpu.SemaphoreType.DMA((2,)),
            pltpu.SemaphoreType.DMA((2, 2)),
            pltpu.SemaphoreType.DMA((2, 2)),
            pltpu.SemaphoreType.DMA((3,)),
        ],
        compiler_params=pltpu.CompilerParams(
            collective_id=3 if back else 1,
            has_side_effects=True,
            vmem_limit_bytes=VMEM_BYTES,
        ),
        cost_estimate=pl.CostEstimate(
            flops=2 * 1024 * WIDTH * cols, bytes_accessed=30_000_000, transcendentals=0
        ),
        name="scatter_back" if back else "scatter_mixed",
    )(*args, weight)


def to_rows(block):
    frames, patches, width = block.shape
    return block.reshape(frames, 8, 8, width).transpose(1, 0, 2, 3).reshape(-1, width)


def from_rows(rows):
    return rows.reshape(8, 2, 8, -1).transpose(1, 0, 2, 3).reshape(2, 64, -1)


def shards(hidden_states, teacher, mod_scale, mod_shift, out_gate, w_qkv, w_out):
    states = to_rows(hidden_states).astype(F32)
    factor = lax.rsqrt(jnp.mean(states * states, -1, keepdims=True) + 1e-06)
    normed = states * factor
    modded = (normed * (1.0 + mod_scale) + mod_shift).astype(BF)
    flat, qkv, factors = gather(modded.reshape(2, HALF, WIDTH), w_qkv, True)
    mixed, attended = scatter([qkv], w_out, False)
    diff = states + out_gate * mixed - to_rows(teacher).astype(F32)
    upstream = (out_gate * diff).astype(BF)
    up_all, grad_att = gather(upstream.reshape(2, HALF, WIDTH), w_out, False)
    out_grad_local = lax.dot_general(
        attended.reshape(1024, LOCAL),
        up_all.reshape(1024, WIDTH),
        (((0,), (0,)), ((), ())),
        preferred_element_type=F32,
    )
    out_grad = lax.psum_scatter(
        out_grad_local.astype(BF), "frame", scatter_dimension=1, tiled=True
    )
    dmod, _, dproj = scatter([qkv, grad_att, factors], w_qkv, True)
    qkv_grad_local = jnp.einsum(
        "td,tch->cdh",
        flat.reshape(1024, WIDTH),
        dproj.reshape(1024, 3, LOCAL),
        preferred_element_type=F32,
    )
    qkv_grad = lax.psum_scatter(
        qkv_grad_local.astype(BF), "frame", scatter_dimension=1, tiled=True
    )
    sums = lax.psum(
        (jnp.sum(dmod * normed, 0), jnp.sum(dmod, 0), jnp.sum(diff * mixed, 0)),
        ("frame", "fsdp"),
    )
    dnorm = dmod * (1.0 + mod_scale)
    grad_hidden = (
        diff + factor * (dnorm - normed * jnp.mean(dnorm * normed, -1, keepdims=True))
    ).astype(BF)
    return (from_rows(grad_hidden), qkv_grad, out_grad, sums[0], sums[1], sums[2])


def solution(mesh):
    in_specs = (
        P("frame", "fsdp", None),
        P("frame", "fsdp", None),
        P(),
        P(),
        P(),
        P(None, None, "fsdp"),
        P("fsdp", None),
    )
    out_specs = (
        P("frame", "fsdp", None),
        P(None, "frame", "fsdp"),
        P("fsdp", "frame"),
        P(),
        P(),
        P(),
    )
    return jax.shard_map(shards, mesh=mesh, in_specs=in_specs, out_specs=out_specs, check_vma=False)
```

time: 1020 us -> 529 us (0.52)
  waiting for transfers between devices: 615 us -> 81.7 us
  Pallas kernels: 0 us -> 288 us
  local copies, waits for them, and re-layouts: 117 us -> 38.4 us
  blocking collectives: 147 us -> 72.5 us
  matrix products: 70.4 us -> 20 us
  other arithmetic: 40 us -> 11.2 us
    pallas_call x0 -> x4, Pallas kernels: none -> 288 us  [the longest x2 161 us: scatter(): pl.pallas_call(functools.partial(scatter_kernel, back), out_shape=shapes,...]
    all_gather x2 -> x0, waiting for transfers between devices: 262 us -> none  [the longest x1 132 us: shards(): gathered = lax.all_gather(modded, 'fsdp', axis=1, tiled=True)]
    reduce_scatter x3 -> x1, waiting for transfers between devices: 260 us -> 73.1 us  [shards(): lax.psum_scatter(out_grad_local.astype(BF), 'frame', scatter_dimension=1,...]
    all_to_all x3 -> x0, blocking collectives: 79.2 us -> none  [the longest x1 38.9 us: shards(): lax.all_to_all(packed, 'frame', split_axis=1, concat_axis=0, tiled=True)]
    unnamed x7 -> x3, waiting for transfers between devices: 66.5 us -> 8.59 us
    dot_general x11 -> x2, matrix products: 65.8 us -> 20 us  [the longest x1 12.1 us: shards(): jnp.einsum('td,tch->cdh', flat.reshape(1024, WIDTH), dproj.reshape(1024,...]
    all_to_all x1 -> x0, waiting for transfers between devices: 26.5 us -> none  [shards(): lax.all_to_all(stacked, 'frame', split_axis=0, concat_axis=1, tiled=True)]
    mul x10 -> x0, local copies, waits for them, and re-layouts: 23.1 us -> none  [the longest x6 14.3 us: head_norm(): return (values * factor, factor)]
  transfers between devices with their start and end apart: 7 -> 2, of which waited for: 7 -> 2; matrix products, arithmetic and copies ran while one was open for 3% -> 3% of each run, Pallas kernels for 0% -> 0%
where the time goes in v1:
time: 529 us; the launch traced here: 527 us
  Pallas kernels  288 us (54%)
  waiting for transfers between devices  81.7 us (15%)
  blocking collectives  72.5 us (14%)
  local copies, waits for them, and re-layouts  38.4 us (7%)
  matrix products  20 us (4%)
  between operations  14.2 us (3%)
  other arithmetic  11.2 us (2%)
    pallas_call x2, Pallas kernels, scatter(): pl.pallas_call(functools.partial(scatter_kernel, back), out_shape=shapes,...  161 us
    pallas_call x2, Pallas kernels, gather(): pl.pallas_call(functools.partial(gather_kernel, project), out_shape=shape...  127 us
    reduce_scatter x1, waiting for transfers between devices, shards(): lax.psum_scatter(out_grad_local.astype(BF), 'frame', scatter_dimension=1,...  73.1 us
    psum x1, blocking collectives, shards(): lax.psum((jnp.sum(dmod * normed, 0), jnp.sum(dmod, 0), jnp.sum(diff * mix...  72.5 us
    unnamed x12, local copies, waits for them, and re-layouts  25.4 us
    dot_general x1, matrix products, shards(): jnp.einsum('td,tch->cdh', flat.reshape(1024, WIDTH), dproj.reshape(1024,...  12.1 us
  transfers between devices with their start and end apart: 2, of which 2 were waited for; matrix products, arithmetic and copies ran while one was open for 3% of the time, Pallas kernels for 0%

profile of v1, /device:TPU:1, one launch (start us, length us, event | category | flops | bytes accessed | tf_op | source)
XLA Modules:
  0.0 526.5 jit_solution(10325995638454229600)
XLA Ops:
  7.2 0.0 reduce-scatter.7.cloned.1.call-start
  7.2 1.4 fusion
  8.6 1.3 convert_bitcast_fusion.1
  9.9 0.1 reshape.113
  10.0 0.1 rsqrt.16
  10.1 1.3 bitcast_convert_fusion
  11.4 1.4 copy.29
  12.7 0.1 copy.27
  12.9 0.6 copy-done.2
  13.4 1.1 add_convert_fusion.1.own
  14.6 72.3 %gather_project.1 = (bf16[2,4,2,64,3072]{4,3,2,1,0:T(8,128)(2,1)}, bf16[4,16,16,1152]{3,2,1,0:T(8,128)(2,1)}, f32[2,4,128,128]{3,2,1,0:T(8,128)}) custom-call(bf16[2,64,3072]{2,1,0:T(8,128)(2,1)} %add_convert_fusion.1.own, bf16[3,3072,384]{2,1,0:T(8,128)(2,1)} %refs_3_.1), custom_call_target="tpu_custom_call" | custom-call | flops 7247757312 | bytes 30000000 | tf_op jit(solution)/shard_map/gather_project/pallas_call | solution.py:247
  86.9 72.9 %scatter_mixed.1 = (f32[128,3072]{1,0:T(8,128)}, bf16[2,4,8,16,384]{4,3,2,1,0:T(8,128)(2,1)}) custom-call(bf16[4,16,16,1152]{3,2,1,0:T(8,128)(2,1)} %get-tuple-element.15.refs_0_, bf16[384,3072]{1,0:T(8,128)(2,1)} %w_hbm.3), custom_call_target="tpu_custom_call" | custom-call | flops 2415919104 | bytes 30000000 | tf_op jit(solution)/shard_map/scatter_mixed/pallas_call | solution.py:484
  159.8 2.3 multiply_reduce_fusion
  162.0 1.0 multiply_convert_fusion
  163.0 54.6 %gather_back.1 = (bf16[2,4,2,64,3072]{4,3,2,1,0:T(8,128)(2,1)}, bf16[4,16,16,384]{3,2,1,0:T(8,128)(2,1)}) custom-call(bf16[2,64,3072]{2,1,0:T(8,128)(2,1)} %bitcast.58, bf16[384,3072]{1,0:T(8,128)(2,1)} %w_hbm.3), custom_call_target="tpu_custom_call" | custom-call | flops 2415919104 | bytes 30000000 | tf_op jit(solution)/shard_map/gather_back/pallas_call | solution.py:247
  217.6 88.6 %scatter_back.1 = (f32[128,3072]{1,0:T(8,128)}, bf16[2,4,8,16,1152]{4,3,2,1,0:T(8,128)(2,1)}, bf16[2,4,128,1152]{3,2,1,0:T(8,128)(2,1)}) custom-call(bf16[4,16,16,1152]{3,2,1,0:T(8,128)(2,1)} %get-tuple-element.15.refs_0_, bf16[4,16,16,384]{3,2,1,0:T(8,128)(2,1)} %get-tuple-element.17.refs_1_, f32[2,4,128,128]{3,2,1,0:T(8,128)} %get-tuple-element.18.refs_2_, ...), custom_call_target="tpu_custom_call" | custom-call | flops 7247757312 | bytes 30000000 | tf_op jit(solution)/shard_map/scatter_back/pallas_call | solution.py:484
  306.2 5.2 copy.32
  311.4 5.1 reshape.102
  316.5 12.1 %convert_bitcast_fusion = bf16[3,3072,384]{1,2,0:T(8,128)(2,1)} fusion(bf16[1024,3,384]{0,2,1:T(8,128)(2,1)} %reshape.102, bf16[1024,3072,1]{1,0,2:T(8,128)(2,1)} %bitcast.61), kind=kOutput, calls=%fused_computation | convolution fusion | flops 7251296256 | bytes 15728640 | tf_op jit(solution)/shard_map/td,tch->cdh/dot_general | solution.py:548
  328.6 14.8 %copy.34 = bf16[3,3072,384]{2,0,1:T(4,128)(2,1)} copy(bf16[3,3072,384]{1,2,0:T(8,128)(2,1)} %convert_bitcast_fusion) | data formatting | bytes 14155776
  343.4 7.8 %copy.37 = bf16[384,8,3,384]{3,1,2,0:T(8,128)(2,1)} copy(bf16[384,8,3,384]{3,2,1,0:T(4,128)(2,1)} %bitcast.53) | data formatting | bytes 14155776
  351.2 0.2 reduce-scatter.5.cloned.1.call-start
  351.4 7.9 %convolution_convert_fusion = bf16[384,3072]{0,1:T(8,128)(2,1)} fusion(bf16[1024,384]{1,0:T(8,128)(2,1)} %bitcast.62, bf16[1024,3072]{1,0:T(8,128)(2,1)} %bitcast.60), kind=kOutput, calls=%fused_computation.1 | convolution fusion | flops 2417098752 | bytes 9437184 | tf_op jit(solution)/shard_map/dot_general | solution.py:538
  359.4 0.1 rsqrt.17
  359.5 2.3 multiply_reduce_fusion.1
  361.7 0.6 add_convert_fusion
  362.3 0.9 copy.39
  363.2 72.5 %all-reduce = (f32[3072]{0:T(1024)}, f32[3072]{0:T(1024)}, f32[3072]{0:T(1024)}) all-reduce(f32[3072]{0:T(1024)S(1)} %get-tuple-element.42, f32[3072]{0:T(1024)S(1)} %get-tuple-element.44, f32[3072]{0:T(1024)S(1)} %get-tuple-element.48), channel_id=1, replica_groups=mesh['frame'=16,'fsdp'=8] {'frame','fsdp'}, use_global_device_ids=true, to_apply=%region_5.0 | all-reduce | flops 9216 | bytes 73728 | tf_op jit(solution)/shard_map/psum | solution.py:557
  435.7 8.6 %reduce-scatter.7.cloned.1.call-done = bf16[192,1152]{1,0:T(8,128)(2,1)} async-done(((bf16[3072,1152]{1,0:T(8,128)(2,1)}), bf16[192,1152]{1,0:T(8,128)(2,1)}) %reduce-scatter.7.cloned.1.call-update) | async-done | bytes 442384
  444.3 1.4 reshape.119
  445.7 0.8 copy.33
  446.6 73.1 %reduce-scatter.5.cloned.1.call-done = bf16[384,192]{0,1:T(8,128)(2,1)} async-done(((bf16[384,3072]{0,1:T(8,128)(2,1)}), bf16[384,192]{0,1:T(8,128)(2,1)}) %reduce-scatter.5.cloned.1.call-update) | async-done | bytes 147472 | tf_op jit(solution)/shard_map/reduce_scatter | solution.py:544
  (13 shorter events, 0.1 us)
Async XLA Ops:
  7.2 2.9 copy-start.3
  7.2 437.1 %reduce-scatter.7.cloned.1.call-start = ((), (), s32[]{:S(2)}) async-start(), calls=%async_computation.3 | async-start | bytes 7520256
  12.7 0.7 copy-start.2
  86.8 72.9 %copy-start.1 = (f32[3072]{0:T(1024)S(1)}, f32[3072]{0:T(1024)}, u32[]{:S(2)}) copy-start(f32[3072]{0:T(1024)} %param.11) | copy-start | bytes 36868
  351.2 168.5 %reduce-scatter.5.cloned.1.call-start = ((), (), s32[]{:S(2)}) async-start(), calls=%async_computation.2 | async-start | bytes 2506752 | tf_op jit(solution)/shard_map/reduce_scatter | solution.py:544
  359.5 2.3 copy-start
Sparse Core Ops, SparseCore 0:
  351.3 92.9 reduce-scatter.6
  449.4 70.2 reduce-scatter.4

commit v2 on v1

--- a/solution.py
+++ b/solution.py
@@ -289,18 +289,181 @@
     return expo / jnp.sum(expo, -1, keepdims=True)
 
 
+class WeightSums:
+    def __init__(self, at, flat, up_all, attended, dproj, result, *scratch):
+        self.at = at
+        self.flat, self.up_all, self.attended, self.dproj = flat, up_all, attended, dproj
+        self.result = result
+        (
+            self.rows, self.turned, self.part, self.twin, self.far, self.near, self.last,
+            self.row_sem, self.t_send, self.t_recv, self.f_send, self.f_recv,
+            self.n_send, self.n_recv, self.l_send, self.l_recv,
+        ) = scratch
+        fr, fs = at.fr, at.fs
+        self.hi = lax.rem(at.group, 2)
+        self.z = lax.div(at.group, 2)
+        self.sibling = (fr + 1 - 2 * at.core, fs)
+        self.over = (fr + 2 - 4 * self.hi, fs)
+        self.up = (lax.rem(fr + 4, 16), fs)
+        self.down = (lax.rem(fr + 12, 16), fs)
+
+    def group(self, off, hi):
+        return 2 * lax.rem(self.z + off, 4) + hi
+
+    def target(self, m):
+        return self.group(far_first(lax.div(m, 2)), lax.rem(m, 2))
+
+    def copies(self, m):
+        cols = pl.ds(pl.multiple_of(self.target(m) * LOCAL, LOCAL), LOCAL)
+        slot = lax.rem(m, 2)
+        return [
+            pltpu.make_async_copy(
+                source.at[:, cols], self.rows.at[slot, i], self.row_sem.at[slot, i]
+            )
+            for i, source in enumerate((self.flat, self.up_all))
+        ]
+
+    def fetch(self, m):
+        for copy in self.copies(m):
+            copy.start()
+
+    def to_twin(self, j):
+        return remote(
+            self.part.at[j, 1 - self.at.core],
+            self.twin.at[j],
+            self.t_send.at[j],
+            self.t_recv.at[j],
+            self.sibling,
+        )
+
+    def mine(self, off, hi):
+        return self.part.at[self.group(off, hi), self.at.core]
+
+    def to_far(self, d):
+        return remote(
+            self.mine(2, d), self.far.at[d], self.f_send.at[d], self.f_recv.at[d],
+            (self.up, self.down)[d],
+        )
+
+    def to_near(self, d, hi):
+        return remote(
+            self.mine((1, 3)[d], hi), self.near.at[d, hi], self.n_send.at[d, hi],
+            self.n_recv.at[d, hi], (self.up, self.down)[d],
+        )
+
+    def tile(self, m):
+        j = self.target(m)
+        slot = lax.rem(m, 2)
+        for copy in self.copies(m):
+            copy.wait()
+
+        @pl.when(m < 7)
+        def _():
+            self.fetch(m + 1)
+
+        self.turned[...] = jnp.transpose(self.rows[slot, 0])
+        for c in range(3):
+            cols = slice(c * LOCAL, (c + 1) * LOCAL)
+            other = self.dproj[:, :, :, cols].reshape(1024, LOCAL)
+            value = jnp.dot(self.turned[...], other, preferred_element_type=F32)
+            self.part[j, :, :, cols] = value.astype(BF).reshape(2, 192, LOCAL)
+        self.turned[...] = jnp.transpose(self.rows[slot, 1])
+        value = jnp.dot(self.turned[...], self.attended[...], preferred_element_type=F32)
+        self.part[j, :, :, 3 * LOCAL :] = value.astype(BF).reshape(2, 192, LOCAL)
+        self.to_twin(j).start()
+
+        @pl.when(m > 0)
+        def _():
+            self.merge(m - 1)
+
+    def add(self, j, other):
+        def rows(i):
+            some = pl.ds(pl.multiple_of(i * 48, 16), 48)
+            held = self.part[j, self.at.core, some, :].astype(F32)
+            self.part[j, self.at.core, some, :] = (held + other[some, :].astype(F32)).astype(BF)
+
+        loop(4, rows)
+
+    def merge(self, m):
+        j = self.target(m)
+        landed(self.twin.at[j], self.t_recv.at[j])
+        self.add(j, self.twin.at[j])
+        for at_step, copy in (
+            (0, lambda: self.to_far(0)),
+            (1, lambda: self.to_far(1)),
+            (3, lambda: self.to_near(0, 1)),
+            (4, lambda: self.to_near(1, 0)),
+        ):
+
+            @pl.when(m == at_step)
+            def _(copy=copy):
+                copy().start()
+
+    def relay(self):
+        for d in range(2):
+            landed(self.far.at[d], self.f_recv.at[d])
+            self.add(self.group((1, 3)[d], d), self.far.at[d])
+            self.to_near(d, d).start()
+
+    def to_last(self):
+        return remote(
+            self.mine(0, 1 - self.hi), self.last, self.l_send, self.l_recv, self.over
+        )
+
+    def finish(self):
+        def arrived(hi):
+            for d in range(2):
+                landed(self.near.at[d, hi], self.n_recv.at[d, hi])
+
+        def both(hi, some):
+            value = self.part[self.group(0, hi), self.at.core, some, :].astype(F32)
+            for d in range(2):
+                value = value + self.near[d, hi, some, :].astype(F32)
+            return value
+
+        arrived(1 - self.hi)
+
+        def rows(i):
+            some = pl.ds(pl.multiple_of(i * 48, 16), 48)
+            self.part[self.group(0, 1 - self.hi), self.at.core, some, :] = both(
+                1 - self.hi, some
+            ).astype(BF)
+
+        loop(4, rows)
+        self.to_last().start()
+        arrived(self.hi)
+        landed(self.last, self.l_recv)
+
+        def end(i):
+            some = pl.ds(pl.multiple_of(i * 48, 16), 48)
+            value = (both(self.hi, some) + self.last[some, :].astype(F32)).astype(BF)
+            for c in range(4):
+                self.result[c, some, :] = value[:, c * LOCAL : (c + 1) * LOCAL]
+
+        loop(4, end)
+        for d in range(2):
+            self.to_far(d).wait_send()
+            for hi in range(2):
+                self.to_near(d, hi).wait_send()
+        self.to_last().wait_send()
+        loop(8, lambda j: self.to_twin(j).wait_send())
+
+
 def scatter_kernel(back, *refs):
     if back:
-        qkv, grad, factors, w_hbm, total, tokens, dproj = refs[:7]
-        refs = refs[7:]
+        qkv, grad, factors, attended, w_hbm, flat, up_all, total, w_grad = refs[:9]
+        refs = refs[9:]
     else:
         qkv, w_hbm, total, tokens = refs[:4]
         refs = refs[4:]
     (
         weight, out, part, mine, from_side, far, near,
         o_send, o_recv, y_send, y_recv, f_send, f_recv, n_send, n_recv, w_sem,
-    ) = refs
+    ) = refs[:16]
     at = Place()
+    if back:
+        tokens, dproj = refs[16:18]
+        sums = WeightSums(at, flat, up_all, attended, dproj, w_grad, *refs[18:])
     if back:
         w_copies = [
             pltpu.make_async_copy(
@@ -312,6 +475,8 @@
         w_copies = [pltpu.make_async_copy(w_hbm, weight, w_sem.at[0])]
     for copy in w_copies:
         copy.start()
+    if back:
+        sums.fetch(0)
     at.meet()
 
     def columns(ref, t, block):
@@ -413,9 +578,15 @@
         remote(mine.at[xl, 1], near.at[1, 1], n_send.at[1, 1], n_recv.at[1, 1], at.left),
     ]
 
+    if back:
+        loop(4, lambda n: take(0, at.along(far_first(n))))
+
     def second(n):
         xi = at.along(far_first(n))
-        take(0, xi)
+        if back:
+            loop(2, lambda q: sums.tile(2 * n + q))
+        else:
+            take(0, xi)
         for h in range(2):
             landed(from_side.at[xi, h], y_recv.at[xi, h])
 
@@ -440,6 +611,8 @@
             near_copies[1].start()
 
     loop(4, second)
+    if back:
+        sums.merge(7)
     for d, xi in ((0, xr), (1, xl)):
         landed(far.at[d], f_recv.at[d])
 
@@ -451,6 +624,8 @@
 
         loop(WIDTH // TILE, tiles)
         near_copies[2 + d].start()
+    if back:
+        sums.relay()
     for d, h in ((0, 1), (1, 0), (0, 0), (1, 1)):
         landed(near.at[d, h], n_recv.at[d, h])
 
@@ -464,6 +639,8 @@
             )
 
     loop(WIDTH // TILE, finish)
+    if back:
+        sums.finish()
     for copy in far_copies + near_copies:
         copy.wait_send()
     for xi in range(4):
@@ -473,37 +650,58 @@
     loop(4, lambda i: landed(out.at[i, pl.ds(0, 15)], o_send.at[i]))
 
 
-def scatter(args, weight, back):
+def scatter(args, weight, back, streamed=()):
     cols = 3 * LOCAL if back else LOCAL
-    shapes = [
-        jax.ShapeDtypeStruct((2 * HALF, WIDTH), F32),
-        jax.ShapeDtypeStruct((2, 4, 8, 16, cols), BF),
+    token_shape = (2, 4, 8, 16, cols)
+    shapes = [jax.ShapeDtypeStruct((2 * HALF, WIDTH), F32)]
+    scratch = [
+        pltpu.VMEM((WIDTH, cols) if back else (LOCAL, WIDTH), BF),
+        pltpu.VMEM((4, 16, 16, cols), BF),
+        pltpu.VMEM((4, 2, HALF, WIDTH), BF),
+        pltpu.VMEM((4, 2, HALF, WIDTH), BF),
+        pltpu.VMEM((4, 2, HALF, WIDTH), BF),
+        pltpu.VMEM((2, HALF, WIDTH), BF),
+        pltpu.VMEM((2, 2, HALF, WIDTH), BF),
+        pltpu.SemaphoreType.DMA((4,)),
+        pltpu.SemaphoreType.DMA((2, 4)),
+        pltpu.SemaphoreType.DMA((4, 2)),
+        pltpu.SemaphoreType.DMA((4, 2)),
+        pltpu.SemaphoreType.DMA((2,)),
+        pltpu.SemaphoreType.DMA((2,)),
+        pltpu.SemaphoreType.DMA((2, 2)),
+        pltpu.SemaphoreType.DMA((2, 2)),
+        pltpu.SemaphoreType.DMA((3,)),
     ]
     if back:
-        shapes.append(jax.ShapeDtypeStruct((2, 4, 2 * HALF, cols), BF))
-    return pl.pallas_call(
-        functools.partial(scatter_kernel, back),
-        out_shape=shapes,
-        in_specs=vmem(len(args)) + [pl.BlockSpec(memory_space=pl.ANY)],
-        out_specs=vmem(len(shapes)),
-        scratch_shapes=[
-            pltpu.VMEM((WIDTH, cols) if back else (LOCAL, WIDTH), BF),
-            pltpu.VMEM((4, 16, 16, cols), BF),
-            pltpu.VMEM((4, 2, HALF, WIDTH), BF),
-            pltpu.VMEM((4, 2, HALF, WIDTH), BF),
-            pltpu.VMEM((4, 2, HALF, WIDTH), BF),
-            pltpu.VMEM((2, HALF, WIDTH), BF),
-            pltpu.VMEM((2, 2, HALF, WIDTH), BF),
-            pltpu.SemaphoreType.DMA((4,)),
-            pltpu.SemaphoreType.DMA((2, 4)),
-            pltpu.SemaphoreType.DMA((4, 2)),
-            pltpu.SemaphoreType.DMA((4, 2)),
+        shapes.append(jax.ShapeDtypeStruct((4, 192, LOCAL), BF))
+        scratch += [
+            pltpu.VMEM(token_shape, BF),
+            pltpu.VMEM((2, 4, 2 * HALF, cols), BF),
+            pltpu.VMEM((2, 2, 1024, LOCAL), BF),
+            pltpu.VMEM((LOCAL, 1024), BF),
+            pltpu.VMEM((8, 2, 192, 4 * LOCAL), BF),
+            pltpu.VMEM((8, 192, 4 * LOCAL), BF),
+            pltpu.VMEM((2, 192, 4 * LOCAL), BF),
+            pltpu.VMEM((2, 2, 192, 4 * LOCAL), BF),
+            pltpu.VMEM((192, 4 * LOCAL), BF),
+            pltpu.SemaphoreType.DMA((2, 2)),
+            pltpu.SemaphoreType.DMA((8,)),
+            pltpu.SemaphoreType.DMA((8,)),
             pltpu.SemaphoreType.DMA((2,)),
             pltpu.SemaphoreType.DMA((2,)),
             pltpu.SemaphoreType.DMA((2, 2)),
             pltpu.SemaphoreType.DMA((2, 2)),
-            pltpu.SemaphoreType.DMA((3,)),
-        ],
+            pltpu.SemaphoreType.DMA,
+            pltpu.SemaphoreType.DMA,
+        ]
+    else:
+        shapes.append(jax.ShapeDtypeStruct(token_shape, BF))
+    return pl.pallas_call(
+        functools.partial(scatter_kernel, back),
+        out_shape=shapes,
+        in_specs=vmem(len(args)) + [pl.BlockSpec(memory_space=pl.ANY)] * (1 + len(streamed)),
+        out_specs=vmem(len(shapes)),
+        scratch_shapes=scratch,
         compiler_params=pltpu.CompilerParams(
             collective_id=3 if back else 1,
             has_side_effects=True,
@@ -513,7 +711,80 @@
             flops=2 * 1024 * WIDTH * cols, bytes_accessed=30_000_000, transcendentals=0
         ),
         name="scatter_back" if back else "scatter_mixed",
-    )(*args, weight)
+    )(*args, weight, *streamed)
+
+
+def total_kernel(own, result, by_head, by_frame, partial, s1, r1, s2, r2, s3, r3):
+    fr = lax.axis_index("frame")
+    fs = lax.axis_index("fsdp")
+    barrier = pltpu.get_barrier_semaphore()
+
+    def head(i):
+        return (fr, lax.rem(fs + i, 8))
+
+    def frame(i):
+        return (lax.rem(fr + i, 16), fs)
+
+    def greet(peer):
+        pl.semaphore_signal(barrier, inc=1, device_id=peer, device_id_type=MESH)
+
+    for i in range(1, 8):
+        greet(head(i))
+    loop(15, lambda i: greet(frame(i + 1)))
+    pl.semaphore_wait(barrier, 22)
+
+    firsts = [
+        remote(own.at[head(i)[1]], by_head.at[fs], s1.at[i], r1, head(i)) for i in range(1, 8)
+    ]
+    for copy in firsts:
+        copy.start()
+    by_head[fs] = own[fs]
+    landed(by_head.at[pl.ds(0, 7)], r1)
+    value = by_head[0]
+    for i in range(1, 8):
+        value = value + by_head[i]
+    partial[...] = value
+    by_frame[fr] = value
+    seconds = [
+        remote(partial, by_frame.at[fr], s2.at[i], r2, frame(i)) for i in range(1, 16)
+    ]
+    for copy in seconds:
+        copy.start()
+    landed(by_frame.at[pl.ds(0, 15)], r2)
+    value = by_frame[0]
+    for i in range(1, 16):
+        value = value + by_frame[i]
+    result[fs] = value
+    thirds = [remote(result.at[fs], result.at[fs], s3.at[i], r3, head(i)) for i in range(1, 8)]
+    for copy in thirds:
+        copy.start()
+    landed(result.at[pl.ds(0, 7)], r3)
+    for copy in firsts + seconds + thirds:
+        copy.wait_send()
+
+
+def total_sums(rows):
+    pieces = jnp.pad(rows.reshape(3, 8, LOCAL).transpose(1, 0, 2), ((0, 0), (0, 5), (0, 0)))
+    result = pl.pallas_call(
+        total_kernel,
+        out_shape=jax.ShapeDtypeStruct((8, 8, LOCAL), F32),
+        in_specs=vmem(1),
+        out_specs=vmem(1)[0],
+        scratch_shapes=[
+            pltpu.VMEM((8, 8, LOCAL), F32),
+            pltpu.VMEM((16, 8, LOCAL), F32),
+            pltpu.VMEM((8, LOCAL), F32),
+            pltpu.SemaphoreType.DMA((8,)),
+            pltpu.SemaphoreType.DMA,
+            pltpu.SemaphoreType.DMA((16,)),
+            pltpu.SemaphoreType.DMA,
+            pltpu.SemaphoreType.DMA((8,)),
+            pltpu.SemaphoreType.DMA,
+        ],
+        compiler_params=pltpu.CompilerParams(collective_id=4, has_side_effects=True),
+        name="total_sums",
+    )(pieces)
+    return result[:, :3].transpose(1, 0, 2).reshape(3, WIDTH)
 
 
 def to_rows(block):
@@ -535,34 +806,20 @@
     diff = states + out_gate * mixed - to_rows(teacher).astype(F32)
     upstream = (out_gate * diff).astype(BF)
     up_all, grad_att = gather(upstream.reshape(2, HALF, WIDTH), w_out, False)
-    out_grad_local = lax.dot_general(
-        attended.reshape(1024, LOCAL),
-        up_all.reshape(1024, WIDTH),
-        (((0,), (0,)), ((), ())),
-        preferred_element_type=F32,
+    dmod, w_grad = scatter(
+        [qkv, grad_att, factors, attended.reshape(1024, LOCAL)],
+        w_qkv,
+        True,
+        (flat.reshape(1024, WIDTH), up_all.reshape(1024, WIDTH)),
     )
-    out_grad = lax.psum_scatter(
-        out_grad_local.astype(BF), "frame", scatter_dimension=1, tiled=True
-    )
-    dmod, _, dproj = scatter([qkv, grad_att, factors], w_qkv, True)
-    qkv_grad_local = jnp.einsum(
-        "td,tch->cdh",
-        flat.reshape(1024, WIDTH),
-        dproj.reshape(1024, 3, LOCAL),
-        preferred_element_type=F32,
-    )
-    qkv_grad = lax.psum_scatter(
-        qkv_grad_local.astype(BF), "frame", scatter_dimension=1, tiled=True
-    )
-    sums = lax.psum(
-        (jnp.sum(dmod * normed, 0), jnp.sum(dmod, 0), jnp.sum(diff * mixed, 0)),
-        ("frame", "fsdp"),
+    sums = total_sums(
+        jnp.stack([jnp.sum(dmod * normed, 0), jnp.sum(dmod, 0), jnp.sum(diff * mixed, 0)])
     )
     dnorm = dmod * (1.0 + mod_scale)
     grad_hidden = (
         diff + factor * (dnorm - normed * jnp.mean(dnorm * normed, -1, keepdims=True))
     ).astype(BF)
-    return (from_rows(grad_hidden), qkv_grad, out_grad, sums[0], sums[1], sums[2])
+    return (from_rows(grad_hidden), w_grad[:3], w_grad[3].T, sums[0], sums[1], sums[2])
 
 
 def solution(mesh):

time: 529 us -> 348 us (0.66)
  waiting for transfers between devices: 81.7 us -> 0 us
  blocking collectives: 72.5 us -> 0 us
  Pallas kernels: 288 us -> 329 us
  local copies, waits for them, and re-layouts: 38.4 us -> 6.97 us
  matrix products: 20 us -> 0 us
  between operations: 14.2 us -> 0.77 us
    reduce_scatter x1 -> x0, waiting for transfers between devices: 73.1 us -> none  [shards(): lax.psum_scatter(out_grad_local.astype(BF), 'frame', scatter_dimension=1,...]
    psum x1 -> x0, blocking collectives: 72.5 us -> none  [shards(): lax.psum((jnp.sum(dmod * normed, 0), jnp.sum(dmod, 0), jnp.sum(diff * mix...]
    unnamed x12 -> x10, local copies, waits for them, and re-layouts: 25.4 us -> 0.74 us
    pallas_call x2, Pallas kernels: 161 us -> 182 us  [scatter(): pl.pallas_call(functools.partial(scatter_kernel, back), out_shape=shapes,...]
    pallas_call x0 -> x1, Pallas kernels: none -> 20.1 us  [total_sums(): pl.pallas_call(total_kernel, out_shape=jax.ShapeDtypeStruct((8, 8, LOCAL)...]
    dot_general x2 -> x0, matrix products: 20 us -> none  [the longest x1 12.1 us: shards(): jnp.einsum('td,tch->cdh', flat.reshape(1024, WIDTH), dproj.reshape(1024,...]
    unnamed x3 -> x0, waiting for transfers between devices: 8.59 us -> none
  transfers between devices with their start and end apart: 2 -> 0, of which waited for: 2 -> 0; matrix products, arithmetic and copies ran while one was open for 3% -> 0% of each run, Pallas kernels for 0% -> 0%
where the time goes in v2:
time: 348 us; the launch traced here: 347 us
  Pallas kernels  329 us (95%)
  other arithmetic  10.7 us (3%)
  local copies, waits for them, and re-layouts  6.97 us (2%)
    pallas_call x2, Pallas kernels, scatter(): pl.pallas_call(functools.partial(scatter_kernel, back), out_shape=shapes,...  182 us
    pallas_call x2, Pallas kernels, gather(): pl.pallas_call(functools.partial(gather_kernel, project), out_shape=shape...  127 us
    pallas_call x1, Pallas kernels, total_sums(): pl.pallas_call(total_kernel, out_shape=jax.ShapeDtypeStruct((8, 8, LOCAL)...  20.1 us

profile of v2, /device:TPU:1, one launch (start us, length us, event | category | flops | bytes accessed | tf_op | source)
XLA Modules:
  0.0 347.4 jit_solution(2724158087081796304)
XLA Ops:
  0.6 1.4 fusion
  2.0 0.1 reshape.123
  2.1 0.1 rsqrt.17
  2.2 0.1 rsqrt.16
  2.3 0.7 broadcast_add_fusion
  3.0 1.3 bitcast_convert_fusion
  4.3 0.0 copy-start.1
  4.3 1.3 copy.15
  5.6 0.1 copy-done.1
  5.7 0.1 convert_bitcast_fusion
  5.8 0.0 copy-start.4
  5.9 0.1 copy.13
  6.0 0.6 copy-done.4
  6.6 1.1 add_convert_fusion.1.own
  7.7 72.3 %gather_project.1 = (bf16[2,4,2,64,3072]{4,3,2,1,0:T(8,128)(2,1)}, bf16[4,16,16,1152]{3,2,1,0:T(8,128)(2,1)}, f32[2,4,128,128]{3,2,1,0:T(8,128)}) custom-call(bf16[2,64,3072]{2,1,0:T(8,128)(2,1)} %add_convert_fusion.1.own, bf16[3,3072,384]{2,1,0:T(8,128)(2,1)} %refs_4_.1), custom_call_target="tpu_custom_call" | custom-call | flops 7247757312 | bytes 30000000 | tf_op jit(solution)/shard_map/gather_project/pallas_call | solution.py:247
  80.0 0.0 copy-start.3
  80.0 72.9 %scatter_mixed.1 = (f32[128,3072]{1,0:T(8,128)}, bf16[2,4,8,16,384]{4,3,2,1,0:T(8,128)(2,1)}) custom-call(bf16[4,16,16,1152]{3,2,1,0:T(8,128)(2,1)} %get-tuple-element.15.refs_0_, bf16[384,3072]{1,0:T(8,128)(2,1)} %w_hbm.3), custom_call_target="tpu_custom_call" | custom-call | flops 2415919104 | bytes 30000000 | tf_op jit(solution)/shard_map/scatter_mixed/pallas_call | solution.py:699
  152.9 0.0 copy-done.3
  152.9 2.3 multiply_reduce_fusion
  155.2 1.0 multiply_convert_fusion
  156.2 54.7 %gather_back.1 = (bf16[2,4,2,64,3072]{4,3,2,1,0:T(8,128)(2,1)}, bf16[4,16,16,384]{3,2,1,0:T(8,128)(2,1)}) custom-call(bf16[2,64,3072]{2,1,0:T(8,128)(2,1)} %bitcast.54, bf16[384,3072]{1,0:T(8,128)(2,1)} %w_hbm.3), custom_call_target="tpu_custom_call" | custom-call | flops 2415919104 | bytes 30000000 | tf_op jit(solution)/shard_map/gather_back/pallas_call | solution.py:247
  210.9 109.0 %scatter_back.1 = (f32[128,3072]{1,0:T(8,128)}, bf16[4,192,384]{2,1,0:T(8,128)(2,1)}) custom-call(bf16[4,16,16,1152]{3,2,1,0:T(8,128)(2,1)} %get-tuple-element.15.refs_0_, bf16[4,16,16,384]{3,2,1,0:T(8,128)(2,1)} %get-tuple-element.17.refs_1_, f32[2,4,128,128]{3,2,1,0:T(8,128)} %get-tuple-element.18.refs_2_, bf16[1024,384]{1,0:T(8,128)(2,1)} %bitcast.64, ...), custom_call_target="tpu_custom_call" | custom-call | flops 7247757312 | bytes 30000000 | tf_op jit(solution)/shard_map/scatter_back/pallas_call | solution.py:699
  319.9 0.0 copy-start
  320.0 2.1 multiply_reduce_fusion.1
  322.1 0.6 add_convert_fusion
  322.7 0.9 copy.19
  323.6 0.7 pad.4.own
  324.3 20.1 %total_sums.1 = f32[8,8,384]{2,1,0:T(8,128)} custom-call(f32[8,8,384]{2,1,0:T(8,128)} %pad.4.own), custom_call_target="tpu_custom_call" | custom-call | tf_op jit(solution)/shard_map/total_sums/pallas_call | solution.py:768
  344.4 0.9 slice_bitcast_fusion.1
  345.3 0.6 fusion.1
  345.9 0.7 slice_bitcast_fusion
  346.6 0.8 slice.21
  (7 shorter events, 0.1 us)
Async XLA Ops:
  4.3 1.4 copy-start.1
  5.8 0.7 copy-start.4
  80.0 73.0 %copy-start.3 = (f32[3072]{0:T(1024)S(1)}, f32[3072]{0:T(1024)}, u32[]{:S(2)}) copy-start(f32[3072]{0:T(1024)} %param.11) | copy-start | bytes 36868
  319.9 2.1 copy-start
  322.7 23.3 %copy-start.2 = (bf16[4,192,384]{2,1,0:T(8,128)(2,1)S(1)}, bf16[4,192,384]{2,1,0:T(8,128)(2,1)}, u32[]{:S(2)}) copy-start(bf16[4,192,384]{2,1,0:T(8,128)(2,1)} %get-tuple-element.23) | copy-start | bytes 1769476

commit v3 on v2

--- a/solution.py
+++ b/solution.py
@@ -79,19 +79,16 @@
     lax.fori_loop(0, count, step, 0)
 
 
-def near_first(p):
-    return 3 * p - lax.div(5 * p * (p - 1), 2) + lax.div(4 * p * (p - 1) * (p - 2), 3)
-
-
-def far_first(p):
-    return 2 - p + lax.div(3 * p * (p - 1), 2) - lax.div(4 * p * (p - 1) * (p - 2), 3)
+def others_first(p):
+    return 2 + p - lax.div(3 * p * (p - 1), 2)
 
 
 def gather_kernel(project, own, w_hbm, *refs):
     if project:
-        full, sent_to, factors, weight, out, x_send, y_send, recv, o_send, o_recv, w_sem = refs
+        kept_all, sent_to, factors, full, weight, out, *sems = refs
     else:
-        full, sent_to, weight, out, x_send, y_send, recv, o_send, o_recv, w_sem = refs
+        kept_all, sent_to, full, weight, out, *sems = refs
+    x_send, y_send, recv, o_send, o_recv, w_sem, keep_sem = sems
     at = Place()
     if project:
         w_copies = [
@@ -106,75 +103,99 @@
         copy.start()
     at.meet()
 
-    def to_right(src, xi, h, n):
-        return remote(src, full.at[0, xi, h], x_send.at[n], recv.at[0, xi, h], at.right)
-
-    def to_left(src, xi, h, n):
-        return remote(src, full.at[0, xi, h], x_send.at[n], recv.at[0, xi, h], at.left)
+    def to_right(slot, src, xi, h, n):
+        return remote(src, full.at[slot, xi, h], x_send.at[n], recv.at[slot, xi, h], at.right)
+
+    def to_left(slot, src, xi, h, n):
+        return remote(src, full.at[slot, xi, h], x_send.at[n], recv.at[slot, xi, h], at.left)
 
     def to_side(src, xi, h, n):
         return remote(src, full.at[1, xi, h], y_send.at[n], recv.at[1, xi, h], at.side[h])
 
     xl, xr, xf = at.along(3), at.along(1), at.along(2)
     first = [
-        to_right(own.at[0], at.x, 0, 0),
-        to_left(own.at[1], at.x, 1, 1),
+        to_right(0, own.at[0], at.x, 0, 0),
+        to_left(0, own.at[1], at.x, 1, 1),
         to_side(own.at[0], at.x, 0, 0),
         to_side(own.at[1], at.x, 1, 1),
-        to_right(own.at[1], at.x, 1, 2),
-        to_left(own.at[0], at.x, 0, 3),
     ]
     for copy in first:
         copy.start()
     full[0, at.x] = own[...]
-    fwd = [
-        to_right(full.at[0, xl, 0], xl, 0, 4),
-        to_left(full.at[0, xr, 1], xr, 1, 5),
-        to_side(full.at[0, xl, 0], xl, 0, 2),
-        to_side(full.at[0, xl, 1], xl, 1, 3),
-        to_side(full.at[0, xr, 0], xr, 0, 4),
-        to_side(full.at[0, xr, 1], xr, 1, 5),
-        to_side(full.at[0, xf, 0], xf, 0, 6),
-        to_side(full.at[0, xf, 1], xf, 1, 7),
-    ]
+    second = [
+        to_right(0, full.at[0, xl, 0], xl, 0, 2),
+        to_left(0, full.at[0, xr, 1], xr, 1, 3),
+    ]
+    if not project:
+        second.append(to_side(full.at[0, xl, 0], xl, 0, 2))
+        second.append(to_side(full.at[0, xr, 1], xr, 1, 3))
+    third = [
+        to_right(0, own.at[1], at.x, 1, 4),
+        to_side(full.at[0, xf, 0], xf, 0, 4),
+        to_left(0, own.at[0], at.x, 0, 5),
+        to_side(full.at[0, xf, 1], xf, 1, 5),
+    ]
+    fourth = [
+        to_right(1, full.at[1, at.x, 1], at.x, 1, 6),
+        to_left(1, full.at[1, at.x, 0], at.x, 0, 7),
+    ]
+    if project:
+        fourth.append(to_right(1, full.at[1, at.x, 0], at.x, 0, 8))
+        fourth.append(to_left(1, full.at[1, at.x, 1], at.x, 1, 9))
     for copy in w_copies:
         copy.wait()
 
     def arrived(slot, xi, h):
         landed(full.at[slot, xi, h], recv.at[slot, xi, h])
 
-    def step(k):
-        slot = lax.div(k, 4)
-        xi = at.along(near_first(lax.rem(k, 4)))
-
+    def early(k):
         @pl.when(k == 1)
         def _():
             arrived(0, xl, 0)
-            fwd[0].start()
-            fwd[2].start()
+            for copy in second[0::2]:
+                copy.start()
             arrived(0, xr, 1)
-            fwd[1].start()
-            fwd[5].start()
+            for copy in second[1::2]:
+                copy.start()
+            arrived(1, at.x, 0)
+            arrived(1, at.x, 1)
+
+        work(k, k, at.x)
+
+    def late(i):
+        slot = lax.div(i, 3)
+        xi = at.along(others_first(lax.rem(i, 3)))
+
+        @pl.when(i == 0)
+        def _():
+            arrived(0, xf, 0)
+            third[0].start()
+            third[1].start()
+            arrived(0, xf, 1)
+            third[2].start()
+            third[3].start()
+
+        @pl.when(i == 1)
+        def _():
             arrived(0, xl, 1)
-            fwd[3].start()
-
-        @pl.when(k == 2)
+            for copy in fourth[0::2]:
+                copy.start()
+
+        @pl.when(i == 2)
         def _():
             arrived(0, xr, 0)
-            fwd[4].start()
-
-        @pl.when(k == 3)
-        def _():
-            arrived(0, xf, 0)
-            fwd[6].start()
-            arrived(0, xf, 1)
-            fwd[7].start()
-
-        @pl.when(k >= 4)
+            for copy in fourth[1::2]:
+                copy.start()
+
+        @pl.when(i >= 3)
         def _():
             arrived(1, xi, 0)
             arrived(1, xi, 1)
 
+        work(i + 2, slot, xi)
+
+    def work(k, slot, xi):
+        pltpu.make_async_copy(full.at[slot, xi], kept_all.at[slot, xi], keep_sem).start()
         tokens = full[slot, xi].reshape(2 * HALF, WIDTH)
         if project:
             both = jnp.dot(tokens, weight[...], preferred_element_type=F32)
@@ -213,9 +234,10 @@
 
         loop(8, give)
 
-    loop(8, step)
-
-    for copy in first + fwd:
+    loop(2, early)
+    loop(6, late)
+
+    for copy in first + second + third + fourth:
         copy.wait_send()
 
     def drain(g):
@@ -228,6 +250,7 @@
             landed(out.at[:, g], o_send.at[g])
 
     loop(8, drain)
+    pltpu.make_async_copy(full, kept_all, keep_sem).wait()
     loop(4, lambda t: landed(sent_to.at[t], o_recv.at[t]))
 
 
@@ -248,16 +271,18 @@
         functools.partial(gather_kernel, project),
         out_shape=shapes,
         in_specs=[pl.BlockSpec(memory_space=pltpu.VMEM), pl.BlockSpec(memory_space=pl.ANY)],
-        out_specs=vmem(len(shapes)),
+        out_specs=[pl.BlockSpec(memory_space=pl.ANY)] + vmem(len(shapes) - 1),
         scratch_shapes=[
+            pltpu.VMEM((2, 4, 2, HALF, WIDTH), BF),
             pltpu.VMEM((WIDTH, cols) if project else (LOCAL, WIDTH), BF),
             pltpu.VMEM((8, 8, 16, cols), BF),
+            pltpu.SemaphoreType.DMA((10,)),
             pltpu.SemaphoreType.DMA((6,)),
-            pltpu.SemaphoreType.DMA((8,)),
             pltpu.SemaphoreType.DMA((2, 4, 2)),
             pltpu.SemaphoreType.DMA((8,)),
             pltpu.SemaphoreType.DMA((4,)),
             pltpu.SemaphoreType.DMA((3,)),
+            pltpu.SemaphoreType.DMA,
         ],
         compiler_params=pltpu.CompilerParams(
             collective_id=0 if project else 2,
@@ -310,22 +335,40 @@
     def group(self, off, hi):
         return 2 * lax.rem(self.z + off, 4) + hi
 
+    def flagged(self, flag):
+        return flag * self.hi + (1 - flag) * (1 - self.hi)
+
     def target(self, m):
-        return self.group(far_first(lax.div(m, 2)), lax.rem(m, 2))
-
-    def copies(self, m):
-        cols = pl.ds(pl.multiple_of(self.target(m) * LOCAL, LOCAL), LOCAL)
+        q, b = lax.div(m, 2), lax.rem(m, 2)
+        inner = lax.div(q * (3 - q), 2)
+        base = 2 - q + lax.div(q * (q - 1), 2) - lax.div(q * (q - 1) * (q - 2), 3)
+        flag = (1 - inner) * b + inner * (q - 1)
+        return self.group(base + 2 * inner * b, self.flagged(flag))
+
+    def load(self, source, j, slot):
+        cols = pl.ds(pl.multiple_of(j * LOCAL, LOCAL), LOCAL)
+        return pltpu.make_async_copy(
+            source.at[:, cols], self.rows.at[slot], self.row_sem.at[slot]
+        )
+
+    def fetch(self, source, j, slot):
+        self.load(source, j, slot).start()
+
+    def out_rows(self, m):
         slot = lax.rem(m, 2)
-        return [
-            pltpu.make_async_copy(
-                source.at[:, cols], self.rows.at[slot, i], self.row_sem.at[slot, i]
-            )
-            for i, source in enumerate((self.flat, self.up_all))
-        ]
-
-    def fetch(self, m):
-        for copy in self.copies(m):
-            copy.start()
+        self.load(self.up_all, m, slot).wait()
+
+        @pl.when(m < 7)
+        def _():
+            self.fetch(self.up_all, m + 1, 1 - slot)
+
+        @pl.when(m == 7)
+        def _():
+            self.fetch(self.flat, self.target(0), 0)
+
+        self.turned[...] = jnp.transpose(self.rows[slot])
+        value = jnp.dot(self.turned[...], self.attended[...], preferred_element_type=F32)
+        self.part[m, :, :, 3 * LOCAL :] = value.astype(BF).reshape(2, 192, LOCAL)
 
     def to_twin(self, j):
         return remote(
@@ -336,115 +379,124 @@
             self.sibling,
         )
 
-    def mine(self, off, hi):
-        return self.part.at[self.group(off, hi), self.at.core]
-
-    def to_far(self, d):
+    def rows_of(self, off, flag, half):
+        j = self.group(off, self.flagged(flag))
+        return self.part.at[j, self.at.core, pl.ds(half * 96, 96)]
+
+    def to_far(self, d, flag):
         return remote(
-            self.mine(2, d), self.far.at[d], self.f_send.at[d], self.f_recv.at[d],
+            self.rows_of(2, flag, d), self.far.at[d, flag], self.f_send.at[d, flag],
+            self.f_recv.at[d, flag], (self.up, self.down)[d],
+        )
+
+    def to_near(self, d, flag, half):
+        return remote(
+            self.rows_of((1, 3)[d], flag, half), self.near.at[d, flag, half],
+            self.n_send.at[d, flag, half], self.n_recv.at[d, flag, half],
             (self.up, self.down)[d],
-        )
-
-    def to_near(self, d, hi):
-        return remote(
-            self.mine((1, 3)[d], hi), self.near.at[d, hi], self.n_send.at[d, hi],
-            self.n_recv.at[d, hi], (self.up, self.down)[d],
         )
 
     def tile(self, m):
         j = self.target(m)
         slot = lax.rem(m, 2)
-        for copy in self.copies(m):
-            copy.wait()
+        self.load(self.flat, j, slot).wait()
 
         @pl.when(m < 7)
         def _():
-            self.fetch(m + 1)
-
-        self.turned[...] = jnp.transpose(self.rows[slot, 0])
+            self.fetch(self.flat, self.target(m + 1), 1 - slot)
+
+        self.turned[...] = jnp.transpose(self.rows[slot])
         for c in range(3):
             cols = slice(c * LOCAL, (c + 1) * LOCAL)
             other = self.dproj[:, :, :, cols].reshape(1024, LOCAL)
             value = jnp.dot(self.turned[...], other, preferred_element_type=F32)
             self.part[j, :, :, cols] = value.astype(BF).reshape(2, 192, LOCAL)
-        self.turned[...] = jnp.transpose(self.rows[slot, 1])
-        value = jnp.dot(self.turned[...], self.attended[...], preferred_element_type=F32)
-        self.part[j, :, :, 3 * LOCAL :] = value.astype(BF).reshape(2, 192, LOCAL)
         self.to_twin(j).start()
 
         @pl.when(m > 0)
         def _():
             self.merge(m - 1)
 
-    def add(self, j, other):
+    def add(self, held, other, count):
         def rows(i):
             some = pl.ds(pl.multiple_of(i * 48, 16), 48)
-            held = self.part[j, self.at.core, some, :].astype(F32)
-            self.part[j, self.at.core, some, :] = (held + other[some, :].astype(F32)).astype(BF)
-
-        loop(4, rows)
+            held[some, :] = (held[some, :].astype(F32) + other[some, :].astype(F32)).astype(BF)
+
+        loop(count, rows)
 
     def merge(self, m):
         j = self.target(m)
         landed(self.twin.at[j], self.t_recv.at[j])
-        self.add(j, self.twin.at[j])
-        for at_step, copy in (
-            (0, lambda: self.to_far(0)),
-            (1, lambda: self.to_far(1)),
-            (3, lambda: self.to_near(0, 1)),
-            (4, lambda: self.to_near(1, 0)),
-        ):
-
-            @pl.when(m == at_step)
-            def _(copy=copy):
-                copy().start()
-
-    def relay(self):
+        self.add(self.part.at[j, self.at.core], self.twin.at[j], 4)
+        for flag in range(2):
+
+            @pl.when(m == flag)
+            def _(flag=flag):
+                for d in range(2):
+                    self.to_far(d, flag).start()
+
+            @pl.when(m == 2 + 2 * flag)
+            def _(flag=flag):
+                if flag == 1:
+                    self.relay(0)
+                self.to_near(0, flag, 1).start()
+
+            @pl.when(m == 3 + 2 * flag)
+            def _(flag=flag):
+                self.to_near(1, flag, 0).start()
+
+    def relay(self, flag):
         for d in range(2):
-            landed(self.far.at[d], self.f_recv.at[d])
-            self.add(self.group((1, 3)[d], d), self.far.at[d])
-            self.to_near(d, d).start()
+            landed(self.far.at[d, flag], self.f_recv.at[d, flag])
+            self.add(self.rows_of((1, 3)[d], flag, d), self.far.at[d, flag], 2)
+            self.to_near(d, flag, d).start()
+
+    def arrived(self, flag):
+        for d in range(2):
+            for half in range(2):
+                landed(self.near.at[d, flag, half], self.n_recv.at[d, flag, half])
+
+    def both(self, flag, half, some):
+        value = self.rows_of(0, flag, half)[some, :].astype(F32)
+        for d in range(2):
+            value = value + self.near[d, flag, half, some, :].astype(F32)
+        return value
 
     def to_last(self):
-        return remote(
-            self.mine(0, 1 - self.hi), self.last, self.l_send, self.l_recv, self.over
-        )
+        source = self.part.at[self.group(0, self.flagged(0)), self.at.core]
+        return remote(source, self.last, self.l_send, self.l_recv, self.over)
+
+    def turn(self):
+        self.arrived(0)
+        for half in range(2):
+            held = self.rows_of(0, 0, half)
+
+            def rows(i, half=half, held=held):
+                some = pl.ds(pl.multiple_of(i * 48, 16), 48)
+                held[some, :] = self.both(0, half, some).astype(BF)
+
+            loop(2, rows)
+        self.to_last().start()
 
     def finish(self):
-        def arrived(hi):
-            for d in range(2):
-                landed(self.near.at[d, hi], self.n_recv.at[d, hi])
-
-        def both(hi, some):
-            value = self.part[self.group(0, hi), self.at.core, some, :].astype(F32)
-            for d in range(2):
-                value = value + self.near[d, hi, some, :].astype(F32)
-            return value
-
-        arrived(1 - self.hi)
-
-        def rows(i):
-            some = pl.ds(pl.multiple_of(i * 48, 16), 48)
-            self.part[self.group(0, 1 - self.hi), self.at.core, some, :] = both(
-                1 - self.hi, some
-            ).astype(BF)
-
-        loop(4, rows)
-        self.to_last().start()
-        arrived(self.hi)
+        self.arrived(1)
         landed(self.last, self.l_recv)
-
-        def end(i):
-            some = pl.ds(pl.multiple_of(i * 48, 16), 48)
-            value = (both(self.hi, some) + self.last[some, :].astype(F32)).astype(BF)
-            for c in range(4):
-                self.result[c, some, :] = value[:, c * LOCAL : (c + 1) * LOCAL]
-
-        loop(4, end)
+        for half in range(2):
+
+            def end(i, half=half):
+                some = pl.ds(pl.multiple_of(i * 48, 16), 48)
+                there = pl.ds(pl.multiple_of(half * 96 + i * 48, 16), 48)
+                value = self.both(1, half, some) + self.last[there, :].astype(F32)
+                value = value.astype(BF)
+                for c in range(4):
+                    self.result[c, there, :] = value[:, c * LOCAL : (c + 1) * LOCAL]
+
+            loop(2, end)
         for d in range(2):
-            self.to_far(d).wait_send()
-            for hi in range(2):
-                self.to_near(d, hi).wait_send()
+            for flag in range(2):
+                self.to_far(d, flag).wait_send()
+                for half in range(2):
+                    self.to_near(d, flag, half).wait_send()
         self.to_last().wait_send()
         loop(8, lambda j: self.to_twin(j).wait_send())
 
@@ -458,12 +510,13 @@
         refs = refs[4:]
     (
         weight, out, part, mine, from_side, far, near,
-        o_send, o_recv, y_send, y_recv, f_send, f_recv, n_send, n_recv, w_sem,
-    ) = refs[:16]
+        passed, o_send, o_recv, y_send, y_recv, f_send, f_recv, n_send, n_recv, p_send, p_recv,
+        w_sem,
+    ) = refs[:19]
     at = Place()
     if back:
-        tokens, dproj = refs[16:18]
-        sums = WeightSums(at, flat, up_all, attended, dproj, w_grad, *refs[18:])
+        tokens, dproj = refs[19:21]
+        sums = WeightSums(at, flat, up_all, attended, dproj, w_grad, *refs[21:])
     if back:
         w_copies = [
             pltpu.make_async_copy(
@@ -476,7 +529,7 @@
     for copy in w_copies:
         copy.start()
     if back:
-        sums.fetch(0)
+        sums.fetch(up_all, 0, 0)
     at.meet()
 
     def columns(ref, t, block):
@@ -530,15 +583,10 @@
         loop(16, give)
 
     loop(4, attend)
+    if back:
+        loop(8, sums.out_rows)
     for copy in w_copies:
         copy.wait()
-
-    def product(slot, xi, j):
-        tile = pl.ds(pl.multiple_of(j * TILE, TILE), TILE)
-        if back:
-            return tile, dot_nt(dproj[slot, xi], weight[tile, :])
-        rows = tokens[slot, xi].reshape(2 * HALF, LOCAL)
-        return tile, jnp.dot(rows, weight[:, tile], preferred_element_type=F32)
 
     def take(slot, xi):
         landed(tokens.at[slot, xi], o_recv.at[slot, xi])
@@ -550,23 +598,48 @@
                     block = (block.astype(F32) * factors[slot, xi, :, j : j + 1]).astype(BF)
                 dproj[slot, xi, :, cols] = block
 
-    def first(n):
-        xi = at.along(far_first(n))
-        take(1, xi)
-
-        def tiles(j):
-            tile, value = product(1, xi, j)
-            part[xi, :, :, tile] = value.astype(BF).reshape(2, HALF, TILE)
-
-        loop(WIDTH // TILE, tiles)
-        for h in range(2):
-            remote(
-                part.at[xi, h], from_side.at[xi, h], y_send.at[xi, h], y_recv.at[xi, h], at.side[h]
-            ).start()
-
-    loop(4, first)
-
     xl, xr, xf = at.along(3), at.along(1), at.along(2)
+
+    def tile_loop(body):
+        loop(WIDTH // TILE, lambda j: body(pl.ds(pl.multiple_of(j * TILE, TILE), TILE)))
+
+    def products(slot, p, into):
+        pair = (at.along(1 + p), at.along(3 - 3 * p))
+        source = dproj if back else tokens
+        rows = jnp.concatenate([source[slot, xi].reshape(2 * HALF, -1) for xi in pair])
+
+        def tiles(tile):
+            if back:
+                value = dot_nt(rows, weight[tile, :])
+            else:
+                value = jnp.dot(rows, weight[:, tile], preferred_element_type=F32)
+            value = value.astype(BF)
+            for n, xi in enumerate(pair):
+                some = value[n * 2 * HALF : (n + 1) * 2 * HALF]
+                into[xi, :, :, tile] = some.reshape(2, HALF, TILE)
+
+        tile_loop(tiles)
+
+    def add(into, xi, h, other):
+        def tiles(tile):
+            value = into[xi, h, :, tile].astype(F32) + other[:, tile].astype(F32)
+            into[xi, h, :, tile] = value.astype(BF)
+
+        tile_loop(tiles)
+
+    def to_side(xi, h):
+        return remote(
+            part.at[xi, h], from_side.at[xi, h], y_send.at[xi, h], y_recv.at[xi, h], at.side[h]
+        )
+
+    def side_arrived(xi, h):
+        landed(from_side.at[xi, h], y_recv.at[xi, h])
+        add(mine, xi, h, from_side.at[xi, h])
+
+    pass_copies = [
+        remote(part.at[xr, 0], passed.at[0], p_send.at[0], p_recv.at[0], at.right),
+        remote(part.at[xl, 1], passed.at[1], p_send.at[1], p_recv.at[1], at.left),
+    ]
     far_copies = [
         remote(mine.at[xf, 0], far.at[0], f_send.at[0], f_recv.at[0], at.right),
         remote(mine.at[xf, 1], far.at[1], f_send.at[1], f_recv.at[1], at.left),
@@ -578,54 +651,65 @@
         remote(mine.at[xl, 1], near.at[1, 1], n_send.at[1, 1], n_recv.at[1, 1], at.left),
     ]
 
-    if back:
-        loop(4, lambda n: take(0, at.along(far_first(n))))
-
-    def second(n):
-        xi = at.along(far_first(n))
+    def first(p):
+        take(1, at.along(1 + p))
+        take(1, at.along(3 - 3 * p))
+        products(1, p, part)
+
+        @pl.when(p == 0)
+        def _():
+            pass_copies[0].start()
+            pass_copies[1].start()
+            to_side(xr, 1).start()
+            to_side(xl, 0).start()
+
+    loop(2, first)
+    if back:
+        loop(4, lambda xi: take(0, xi))
+        loop(2, sums.tile)
+
+    def second(p):
+        if not back:
+            take(0, at.along(1 + p))
+            take(0, at.along(3 - 3 * p))
+        products(0, p, mine)
+
+        @pl.when(p == 0)
+        def _():
+            for h in range(2):
+                to_side((xl, xr)[h], h).wait_send()
+                to_side(xf, h).start()
+            for h in range(2):
+                landed(passed.at[h], p_recv.at[h])
+                add(part, at.x, h, passed.at[h])
+            side_arrived(xr, 1)
+            near_copies[0].start()
+            side_arrived(xl, 0)
+            near_copies[1].start()
+
         if back:
-            loop(2, lambda q: sums.tile(2 * n + q))
-        else:
-            take(0, xi)
-        for h in range(2):
-            landed(from_side.at[xi, h], y_recv.at[xi, h])
-
-        def tiles(j):
-            tile, value = product(0, xi, j)
-            other = from_side[xi, :, :, tile].astype(F32).reshape(2 * HALF, TILE)
-            mine[xi, :, :, tile] = (value + other).astype(BF).reshape(2, HALF, TILE)
-
-        loop(WIDTH // TILE, tiles)
-
-        @pl.when(n == 0)
-        def _():
-            far_copies[0].start()
-            far_copies[1].start()
-
-        @pl.when(n == 1)
-        def _():
-            near_copies[0].start()
-
-        @pl.when(n == 2)
-        def _():
-            near_copies[1].start()
-
-    loop(4, second)
-    if back:
+            loop(2, lambda q: sums.tile(2 + 2 * p + q))
+
+    loop(2, second)
+    for h in range(2):
+        to_side(xf, h).wait_send()
+        to_side(at.x, h).start()
+    for h in range(2):
+        side_arrived(xf, h)
+        far_copies[h].start()
+    if back:
+        loop(2, lambda q: sums.tile(6 + q))
         sums.merge(7)
     for d, xi in ((0, xr), (1, xl)):
         landed(far.at[d], f_recv.at[d])
-
-        def tiles(j, d=d, xi=xi):
-            tile = pl.ds(pl.multiple_of(j * TILE, TILE), TILE)
-            mine[xi, d, :, tile] = (
-                mine[xi, d, :, tile].astype(F32) + far[d, :, tile].astype(F32)
-            ).astype(BF)
-
-        loop(WIDTH // TILE, tiles)
+        add(mine, xi, d, far.at[d])
         near_copies[2 + d].start()
     if back:
-        sums.relay()
+        sums.relay(1)
+    for h in range(2):
+        side_arrived(at.x, h)
+    if back:
+        sums.turn()
     for d, h in ((0, 1), (1, 0), (0, 0), (1, 1)):
         landed(near.at[d, h], n_recv.at[d, h])
 
@@ -641,11 +725,10 @@
     loop(WIDTH // TILE, finish)
     if back:
         sums.finish()
-    for copy in far_copies + near_copies:
+    for copy in pass_copies + far_copies + near_copies:
         copy.wait_send()
-    for xi in range(4):
-        for h in range(2):
-            landed(part.at[xi, h], y_send.at[xi, h])
+    for h in range(2):
+        to_side(at.x, h).wait_send()
 
     loop(4, lambda i: landed(out.at[i, pl.ds(0, 15)], o_send.at[i]))
 
@@ -662,6 +745,7 @@
         pltpu.VMEM((4, 2, HALF, WIDTH), BF),
         pltpu.VMEM((2, HALF, WIDTH), BF),
         pltpu.VMEM((2, 2, HALF, WIDTH), BF),
+        pltpu.VMEM((2, HALF, WIDTH), BF),
         pltpu.SemaphoreType.DMA((4,)),
         pltpu.SemaphoreType.DMA((2, 4)),
         pltpu.SemaphoreType.DMA((4, 2)),
@@ -670,6 +754,8 @@
         pltpu.SemaphoreType.DMA((2,)),
         pltpu.SemaphoreType.DMA((2, 2)),
         pltpu.SemaphoreType.DMA((2, 2)),
+        pltpu.SemaphoreType.DMA((2,)),
+        pltpu.SemaphoreType.DMA((2,)),
         pltpu.SemaphoreType.DMA((3,)),
     ]
     if back:
@@ -677,20 +763,20 @@
         scratch += [
             pltpu.VMEM(token_shape, BF),
             pltpu.VMEM((2, 4, 2 * HALF, cols), BF),
-            pltpu.VMEM((2, 2, 1024, LOCAL), BF),
+            pltpu.VMEM((2, 1024, LOCAL), BF),
             pltpu.VMEM((LOCAL, 1024), BF),
             pltpu.VMEM((8, 2, 192, 4 * LOCAL), BF),
             pltpu.VMEM((8, 192, 4 * LOCAL), BF),
-            pltpu.VMEM((2, 192, 4 * LOCAL), BF),
-            pltpu.VMEM((2, 2, 192, 4 * LOCAL), BF),
+            pltpu.VMEM((2, 2, 96, 4 * LOCAL), BF),
+            pltpu.VMEM((2, 2, 2, 96, 4 * LOCAL), BF),
             pltpu.VMEM((192, 4 * LOCAL), BF),
-            pltpu.SemaphoreType.DMA((2, 2)),
+            pltpu.SemaphoreType.DMA((2,)),
             pltpu.SemaphoreType.DMA((8,)),
             pltpu.SemaphoreType.DMA((8,)),
-            pltpu.SemaphoreType.DMA((2,)),
-            pltpu.SemaphoreType.DMA((2,)),
             pltpu.SemaphoreType.DMA((2, 2)),
             pltpu.SemaphoreType.DMA((2, 2)),
+            pltpu.SemaphoreType.DMA((2, 2, 2)),
+            pltpu.SemaphoreType.DMA((2, 2, 2)),
             pltpu.SemaphoreType.DMA,
             pltpu.SemaphoreType.DMA,
         ]

time: 348 us -> 301 us (0.86)
  Pallas kernels: 329 us -> 281 us
    pallas_call x2, Pallas kernels: 182 us -> 143 us  [scatter(): pl.pallas_call(functools.partial(scatter_kernel, back), out_shape=shapes,...]
    pallas_call x2, Pallas kernels: 127 us -> 118 us  [gather(): pl.pallas_call(functools.partial(gather_kernel, project), out_shape=shape...]
where the time goes in v3:
time: 301 us; the launch traced here: 300 us
  Pallas kernels  281 us (93%)
  other arithmetic  10.7 us (4%)
  local copies, waits for them, and re-layouts  6.97 us (2%)
    pallas_call x2, Pallas kernels, scatter(): pl.pallas_call(functools.partial(scatter_kernel, back), out_shape=shapes,...  143 us
    pallas_call x2, Pallas kernels, gather(): pl.pallas_call(functools.partial(gather_kernel, project), out_shape=shape...  118 us
    pallas_call x1, Pallas kernels, total_sums(): pl.pallas_call(total_kernel, out_shape=jax.ShapeDtypeStruct((8, 8, LOCAL)...  20.4 us

profile of v3, /device:TPU:1, one launch (start us, length us, event | category | flops | bytes accessed | tf_op | source)
XLA Modules:
  0.0 299.8 jit_solution(12227988630718598796)
XLA Ops:
  0.6 1.4 fusion
  2.0 0.1 reshape.123
  2.1 0.1 rsqrt.17
  2.2 0.1 rsqrt.16
  2.3 0.7 broadcast_add_fusion
  3.0 1.3 bitcast_convert_fusion
  4.3 0.0 copy-start.1
  4.3 1.3 copy.15
  5.6 0.1 copy-done.1
  5.7 0.1 convert_bitcast_fusion
  5.8 0.0 copy-start.4
  5.9 0.1 copy.13
  6.0 0.6 copy-done.4
  6.6 1.1 add_convert_fusion.1.own
  7.7 65.8 %gather_project.1 = (bf16[2,4,2,64,3072]{4,3,2,1,0:T(8,128)(2,1)}, bf16[4,16,16,1152]{3,2,1,0:T(8,128)(2,1)}, f32[2,4,128,128]{3,2,1,0:T(8,128)}) custom-call(bf16[2,64,3072]{2,1,0:T(8,128)(2,1)} %add_convert_fusion.1.own, bf16[3,3072,384]{2,1,0:T(8,128)(2,1)} %refs_4_.1), custom_call_target="tpu_custom_call" | custom-call | flops 7247757312 | bytes 30000000 | tf_op jit(solution)/shard_map/gather_project/pallas_call | solution.py:270
  73.5 0.0 copy-start.3
  73.5 58.3 %scatter_mixed.1 = (f32[128,3072]{1,0:T(8,128)}, bf16[2,4,8,16,384]{4,3,2,1,0:T(8,128)(2,1)}) custom-call(bf16[4,16,16,1152]{3,2,1,0:T(8,128)(2,1)} %get-tuple-element.15.refs_0_, bf16[384,3072]{1,0:T(8,128)(2,1)} %w_hbm.3), custom_call_target="tpu_custom_call" | custom-call | flops 2415919104 | bytes 30000000 | tf_op jit(solution)/shard_map/scatter_mixed/pallas_call | solution.py:785
  131.9 2.3 multiply_reduce_fusion
  134.1 1.0 multiply_convert_fusion
  135.1 52.2 %gather_back.1 = (bf16[2,4,2,64,3072]{4,3,2,1,0:T(8,128)(2,1)}, bf16[4,16,16,384]{3,2,1,0:T(8,128)(2,1)}) custom-call(bf16[2,64,3072]{2,1,0:T(8,128)(2,1)} %bitcast.54, bf16[384,3072]{1,0:T(8,128)(2,1)} %w_hbm.3), custom_call_target="tpu_custom_call" | custom-call | flops 2415919104 | bytes 30000000 | tf_op jit(solution)/shard_map/gather_back/pallas_call | solution.py:270
  187.4 84.7 %scatter_back.1 = (f32[128,3072]{1,0:T(8,128)}, bf16[4,192,384]{2,1,0:T(8,128)(2,1)}) custom-call(bf16[4,16,16,1152]{3,2,1,0:T(8,128)(2,1)} %get-tuple-element.15.refs_0_, bf16[4,16,16,384]{3,2,1,0:T(8,128)(2,1)} %get-tuple-element.17.refs_1_, f32[2,4,128,128]{3,2,1,0:T(8,128)} %get-tuple-element.18.refs_2_, bf16[1024,384]{1,0:T(8,128)(2,1)} %bitcast.64, ...), custom_call_target="tpu_custom_call" | custom-call | flops 7247757312 | bytes 30000000 | tf_op jit(solution)/shard_map/scatter_back/pallas_call | solution.py:785
  272.1 0.0 copy-start
  272.1 2.1 multiply_reduce_fusion.1
  274.2 0.0 copy-done
  274.2 0.6 add_convert_fusion
  274.8 0.9 copy.19
  275.8 0.7 pad.4.own
  276.4 20.4 %total_sums.1 = f32[8,8,384]{2,1,0:T(8,128)} custom-call(f32[8,8,384]{2,1,0:T(8,128)} %pad.4.own), custom_call_target="tpu_custom_call" | custom-call | tf_op jit(solution)/shard_map/total_sums/pallas_call | solution.py:854
  296.8 0.9 slice_bitcast_fusion.1
  297.7 0.6 fusion.1
  298.4 0.7 slice_bitcast_fusion
  299.0 0.8 slice.21
  (7 shorter events, 0.1 us)
Async XLA Ops:
  4.3 1.4 copy-start.1
  5.8 0.7 copy-start.4
  73.5 58.4 %copy-start.3 = (f32[3072]{0:T(1024)S(1)}, f32[3072]{0:T(1024)}, u32[]{:S(2)}) copy-start(f32[3072]{0:T(1024)} %param.11) | copy-start | bytes 36868
  272.1 2.1 copy-start
  274.8 23.5 %copy-start.2 = (bf16[4,192,384]{2,1,0:T(8,128)(2,1)S(1)}, bf16[4,192,384]{2,1,0:T(8,128)(2,1)}, u32[]{:S(2)}) copy-start(bf16[4,192,384]{2,1,0:T(8,128)(2,1)} %get-tuple-element.23) | copy-start | bytes 1769476

commit v4 on v3

--- a/solution.py
+++ b/solution.py
@@ -38,22 +38,23 @@
     def along(self, off):
         return lax.rem(self.x + off, 4)
 
-    def meet(self):
+    def greet(self, heads):
         barrier = pltpu.get_barrier_semaphore()
-        for peer in (self.right, self.left) + self.side:
+
+        def signal(peer):
             pl.semaphore_signal(barrier, inc=1, device_id=peer, device_id_type=MESH)
 
-        def greet(step, carry):
-            pl.semaphore_signal(
-                barrier,
-                inc=1,
-                device_id=(lax.rem(self.fr + step, 16), self.fs),
-                device_id_type=MESH,
-            )
-            return carry
-
-        lax.fori_loop(1, 16, greet, 0)
-        pl.semaphore_wait(barrier, 19)
+        signal(self.side[1])
+        if heads:
+            for step in range(1, 8):
+                signal((self.fr, lax.rem(self.fs + step, 8)))
+        else:
+            for peer in (self.right, self.left, self.side[0]):
+                signal(peer)
+        loop(15, lambda i: signal((lax.rem(self.fr + i + 1, 16), self.fs)))
+
+    def met(self, heads):
+        pl.semaphore_wait(pltpu.get_barrier_semaphore(), 23 if heads else 19)
 
 
 def remote(src, dst, send_sem, recv_sem, device):
@@ -83,25 +84,22 @@
     return 2 + p - lax.div(3 * p * (p - 1), 2)
 
 
-def gather_kernel(project, own, w_hbm, *refs):
-    if project:
-        kept_all, sent_to, factors, full, weight, out, *sems = refs
-    else:
-        kept_all, sent_to, full, weight, out, *sems = refs
-    x_send, y_send, recv, o_send, o_recv, w_sem, keep_sem = sems
-    at = Place()
-    if project:
-        w_copies = [
-            pltpu.make_async_copy(
-                w_hbm.at[c], weight.at[:, pl.ds(c * LOCAL, LOCAL)], w_sem.at[c]
-            )
+def load_weight(w_hbm, weight, sem):
+    if len(w_hbm.shape) == 3:
+        copies = [
+            pltpu.make_async_copy(w_hbm.at[c], weight.at[:, pl.ds(c * LOCAL, LOCAL)], sem.at[c])
             for c in range(3)
         ]
     else:
-        w_copies = [pltpu.make_async_copy(w_hbm, weight, w_sem.at[0])]
-    for copy in w_copies:
+        copies = [pltpu.make_async_copy(w_hbm, weight, sem.at[0])]
+    for copy in copies:
         copy.start()
-    at.meet()
+    return copies
+
+
+def gather_phase(at, own, weight, w_copies, kept_all, sent_to, factors, scratch, between=None):
+    full, out, x_send, y_send, recv, o_send, o_recv, keep_sem = scratch
+    project = factors is not None
 
     def to_right(slot, src, xi, h, n):
         return remote(src, full.at[slot, xi, h], x_send.at[n], recv.at[slot, xi, h], at.right)
@@ -187,6 +185,9 @@
             for copy in fourth[1::2]:
                 copy.start()
 
+        if between is not None:
+            pl.when(i == 4)(between)
+
         @pl.when(i >= 3)
         def _():
             arrived(1, xi, 0)
@@ -237,9 +238,6 @@
     loop(2, early)
     loop(6, late)
 
-    for copy in first + second + third + fourth:
-        copy.wait_send()
-
     def drain(g):
         @pl.when(g == at.group)
         def _():
@@ -249,49 +247,34 @@
         def _():
             landed(out.at[:, g], o_send.at[g])
 
-    loop(8, drain)
-    pltpu.make_async_copy(full, kept_all, keep_sem).wait()
-    loop(4, lambda t: landed(sent_to.at[t], o_recv.at[t]))
+    def end():
+        for copy in first + second + third + fourth:
+            copy.wait_send()
+        loop(8, drain)
+        pltpu.make_async_copy(full, kept_all, keep_sem).wait()
+
+    return end
+
+
+def gather_scratch(cols):
+    return [
+        pltpu.VMEM((2, 4, 2, HALF, WIDTH), BF),
+        pltpu.VMEM((8, 8, 16, cols), BF),
+        pltpu.SemaphoreType.DMA((10,)),
+        pltpu.SemaphoreType.DMA((6,)),
+        pltpu.SemaphoreType.DMA((2, 4, 2)),
+        pltpu.SemaphoreType.DMA((8,)),
+        pltpu.SemaphoreType.DMA((4,)),
+        pltpu.SemaphoreType.DMA,
+    ]
 
 
 def vmem(count):
     return [pl.BlockSpec(memory_space=pltpu.VMEM)] * count
 
 
-def gather(own, weight, project):
-    cols = 3 * LOCAL if project else LOCAL
-    shapes = [
-        jax.ShapeDtypeStruct((2, 4, 2, HALF, WIDTH), BF),
-        jax.ShapeDtypeStruct((4, 16, 16, cols), BF),
-    ]
-    if project:
-        shapes.append(jax.ShapeDtypeStruct((2, 4, 2 * HALF, HEAD_DIM), F32))
-    flops = 2 * 1024 * WIDTH * cols
-    return pl.pallas_call(
-        functools.partial(gather_kernel, project),
-        out_shape=shapes,
-        in_specs=[pl.BlockSpec(memory_space=pltpu.VMEM), pl.BlockSpec(memory_space=pl.ANY)],
-        out_specs=[pl.BlockSpec(memory_space=pl.ANY)] + vmem(len(shapes) - 1),
-        scratch_shapes=[
-            pltpu.VMEM((2, 4, 2, HALF, WIDTH), BF),
-            pltpu.VMEM((WIDTH, cols) if project else (LOCAL, WIDTH), BF),
-            pltpu.VMEM((8, 8, 16, cols), BF),
-            pltpu.SemaphoreType.DMA((10,)),
-            pltpu.SemaphoreType.DMA((6,)),
-            pltpu.SemaphoreType.DMA((2, 4, 2)),
-            pltpu.SemaphoreType.DMA((8,)),
-            pltpu.SemaphoreType.DMA((4,)),
-            pltpu.SemaphoreType.DMA((3,)),
-            pltpu.SemaphoreType.DMA,
-        ],
-        compiler_params=pltpu.CompilerParams(
-            collective_id=0 if project else 2,
-            has_side_effects=True,
-            vmem_limit_bytes=VMEM_BYTES,
-        ),
-        cost_estimate=pl.CostEstimate(flops=flops, bytes_accessed=30_000_000, transcendentals=0),
-        name="gather_project" if project else "gather_back",
-    )(own, weight)
+def anywhere(count):
+    return [pl.BlockSpec(memory_space=pl.ANY)] * count
 
 
 def same_patch():
@@ -501,57 +484,47 @@
         loop(8, lambda j: self.to_twin(j).wait_send())
 
 
-def scatter_kernel(back, *refs):
-    if back:
-        qkv, grad, factors, attended, w_hbm, flat, up_all, total, w_grad = refs[:9]
-        refs = refs[9:]
-    else:
-        qkv, w_hbm, total, tokens = refs[:4]
-        refs = refs[4:]
-    (
-        weight, out, part, mine, from_side, far, near,
-        passed, o_send, o_recv, y_send, y_recv, f_send, f_recv, n_send, n_recv, p_send, p_recv,
-        w_sem,
-    ) = refs[:19]
-    at = Place()
-    if back:
-        tokens, dproj = refs[19:21]
-        sums = WeightSums(at, flat, up_all, attended, dproj, w_grad, *refs[21:])
-    if back:
-        w_copies = [
-            pltpu.make_async_copy(
-                w_hbm.at[c], weight.at[:, pl.ds(c * LOCAL, LOCAL)], w_sem.at[c]
-            )
-            for c in range(3)
-        ]
-    else:
-        w_copies = [pltpu.make_async_copy(w_hbm, weight, w_sem.at[0])]
-    for copy in w_copies:
-        copy.start()
-    if back:
-        sums.fetch(up_all, 0, 0)
-    at.meet()
-
-    def columns(ref, t, block):
-        return ref[t, :, :, block * HEAD_DIM : (block + 1) * HEAD_DIM].reshape(256, HEAD_DIM)
-
-    def put(i, block, value):
-        out[i, :, :, block * HEAD_DIM : (block + 1) * HEAD_DIM] = value.astype(BF).reshape(
-            16, 16, HEAD_DIM
-        )
-
-    def attend(i):
-        slot = 1 - lax.div(i, 2)
-        xh = lax.rem(i, 2)
+def tile_loop(body):
+    loop(WIDTH // TILE, lambda j: body(pl.ds(pl.multiple_of(j * TILE, TILE), TILE)))
+
+
+class Scatter:
+    def __init__(self, at, qkv, qkv_sem, grad, weight, tokens, dproj, factors, scratch):
+        self.at, self.qkv, self.qkv_sem, self.grad = at, qkv, qkv_sem, grad
+        self.weight, self.tokens, self.dproj, self.factors = weight, tokens, dproj, factors
+        (
+            self.out, self.part, self.own, self.from_side, self.far, self.near, self.passed,
+            self.o_send, self.o_recv, self.y_send, self.y_recv, self.f_send, self.f_recv,
+            self.n_send, self.n_recv, self.p_send, self.p_recv,
+        ) = scratch
+        self.back = grad is not None
+        self.xl, self.xr, self.xf = at.along(3), at.along(1), at.along(2)
+
+    def put(self, i, block, value):
+        cols = slice(block * HEAD_DIM, (block + 1) * HEAD_DIM)
+        self.out[i, :, :, cols] = value.astype(BF).reshape(16, 16, HEAD_DIM)
+
+    def attend(self, i):
+        at, put = self.at, self.put
+        slot = lax.div(i, 2)
+        if self.back:
+            slot = 1 - slot
+        xh = lax.rem(lax.div(at.x, 2) + i, 2)
         t = 2 * xh + lax.rem(at.lo + slot, 2)
+        if self.qkv_sem is not None:
+            landed(self.qkv.at[t], self.qkv_sem.at[t])
+
+        def columns(ref, block):
+            return ref[t, :, :, block * HEAD_DIM : (block + 1) * HEAD_DIM].reshape(256, HEAD_DIM)
+
         for h in range(HEADS):
-            query, key, value = (columns(qkv, t, c * HEADS + h) for c in range(3))
+            query, key, value = (columns(self.qkv, c * HEADS + h) for c in range(3))
             probs = softmax(query, key)
             low = probs.astype(BF)
-            if not back:
+            if not self.back:
                 put(i, h, jnp.dot(low, value, preferred_element_type=F32))
                 continue
-            grad_in = columns(grad, t, h)
+            grad_in = columns(self.grad, h)
             dprob = dot_nt(grad_in, value)
             put(i, 2 * HEADS + h, dot_tn(low, grad_in))
             dscore = (probs * (dprob - jnp.sum(probs * dprob, -1, keepdims=True))).astype(BF)
@@ -569,50 +542,44 @@
         xi = 2 * xh + at.core
 
         def give(f):
-            src = out.at[i, f]
-            dst = tokens.at[slot, xi, at.group]
+            src = self.out.at[i, f]
+            dst = self.tokens.at[slot, xi, at.group]
 
             @pl.when(f == at.fr)
             def _():
-                pltpu.make_async_copy(src, dst, o_recv.at[slot, xi]).start()
+                pltpu.make_async_copy(src, dst, self.o_recv.at[slot, xi]).start()
 
             @pl.when(f != at.fr)
             def _():
-                remote(src, dst, o_send.at[i], o_recv.at[slot, xi], (f, at.fs)).start()
+                remote(
+                    src, dst, self.o_send.at[i], self.o_recv.at[slot, xi], (f, at.fs)
+                ).start()
 
         loop(16, give)
 
-    loop(4, attend)
-    if back:
-        loop(8, sums.out_rows)
-    for copy in w_copies:
-        copy.wait()
-
-    def take(slot, xi):
-        landed(tokens.at[slot, xi], o_recv.at[slot, xi])
-        if back:
+    def take(self, slot, xi):
+        landed(self.tokens.at[slot, xi], self.o_recv.at[slot, xi])
+        if self.back:
             for j in range(3 * HEADS):
                 cols = slice(j * HEAD_DIM, (j + 1) * HEAD_DIM)
-                block = tokens[slot, xi, :, :, cols].reshape(2 * HALF, HEAD_DIM)
+                block = self.tokens[slot, xi, :, :, cols].reshape(2 * HALF, HEAD_DIM)
                 if j < 2 * HEADS:
-                    block = (block.astype(F32) * factors[slot, xi, :, j : j + 1]).astype(BF)
-                dproj[slot, xi, :, cols] = block
-
-    xl, xr, xf = at.along(3), at.along(1), at.along(2)
-
-    def tile_loop(body):
-        loop(WIDTH // TILE, lambda j: body(pl.ds(pl.multiple_of(j * TILE, TILE), TILE)))
-
-    def products(slot, p, into):
-        pair = (at.along(1 + p), at.along(3 - 3 * p))
-        source = dproj if back else tokens
+                    block = (block.astype(F32) * self.factors[slot, xi, :, j : j + 1]).astype(BF)
+                self.dproj[slot, xi, :, cols] = block
+
+    def pair(self, p):
+        return self.at.along(1 + p), self.at.along(3 - 3 * p)
+
+    def products(self, slot, p, into):
+        pair = self.pair(p)
+        source = self.dproj if self.back else self.tokens
         rows = jnp.concatenate([source[slot, xi].reshape(2 * HALF, -1) for xi in pair])
 
         def tiles(tile):
-            if back:
-                value = dot_nt(rows, weight[tile, :])
+            if self.back:
+                value = dot_nt(rows, self.weight[tile, :])
             else:
-                value = jnp.dot(rows, weight[:, tile], preferred_element_type=F32)
+                value = jnp.dot(rows, self.weight[:, tile], preferred_element_type=F32)
             value = value.astype(BF)
             for n, xi in enumerate(pair):
                 some = value[n * 2 * HALF : (n + 1) * 2 * HALF]
@@ -620,125 +587,161 @@
 
         tile_loop(tiles)
 
-    def add(into, xi, h, other):
+    def add(self, into, xi, h, other):
         def tiles(tile):
             value = into[xi, h, :, tile].astype(F32) + other[:, tile].astype(F32)
             into[xi, h, :, tile] = value.astype(BF)
 
         tile_loop(tiles)
 
-    def to_side(xi, h):
+    def to_side(self, xi, h):
         return remote(
-            part.at[xi, h], from_side.at[xi, h], y_send.at[xi, h], y_recv.at[xi, h], at.side[h]
+            self.part.at[xi, h], self.from_side.at[xi, h], self.y_send.at[xi, h],
+            self.y_recv.at[xi, h], self.at.side[h],
         )
 
-    def side_arrived(xi, h):
-        landed(from_side.at[xi, h], y_recv.at[xi, h])
-        add(mine, xi, h, from_side.at[xi, h])
-
-    pass_copies = [
-        remote(part.at[xr, 0], passed.at[0], p_send.at[0], p_recv.at[0], at.right),
-        remote(part.at[xl, 1], passed.at[1], p_send.at[1], p_recv.at[1], at.left),
-    ]
-    far_copies = [
-        remote(mine.at[xf, 0], far.at[0], f_send.at[0], f_recv.at[0], at.right),
-        remote(mine.at[xf, 1], far.at[1], f_send.at[1], f_recv.at[1], at.left),
-    ]
-    near_copies = [
-        remote(mine.at[xr, 1], near.at[0, 1], n_send.at[0, 1], n_recv.at[0, 1], at.right),
-        remote(mine.at[xl, 0], near.at[1, 0], n_send.at[1, 0], n_recv.at[1, 0], at.left),
-        remote(mine.at[xr, 0], near.at[0, 0], n_send.at[0, 0], n_recv.at[0, 0], at.right),
-        remote(mine.at[xl, 1], near.at[1, 1], n_send.at[1, 1], n_recv.at[1, 1], at.left),
-    ]
-
-    def first(p):
-        take(1, at.along(1 + p))
-        take(1, at.along(3 - 3 * p))
-        products(1, p, part)
-
-        @pl.when(p == 0)
-        def _():
-            pass_copies[0].start()
-            pass_copies[1].start()
-            to_side(xr, 1).start()
-            to_side(xl, 0).start()
-
-    loop(2, first)
-    if back:
-        loop(4, lambda xi: take(0, xi))
+    def side_arrived(self, xi, h):
+        landed(self.from_side.at[xi, h], self.y_recv.at[xi, h])
+        self.add(self.own, xi, h, self.from_side.at[xi, h])
+
+    def way(self, d):
+        return (self.at.right, self.at.left)[d]
+
+    def pass_on(self, d):
+        source = self.part.at[(self.xr, self.xl)[d], d]
+        return remote(source, self.passed.at[d], self.p_send.at[d], self.p_recv.at[d], self.way(d))
+
+    def to_far(self, d):
+        source = self.own.at[self.xf, d]
+        return remote(source, self.far.at[d], self.f_send.at[d], self.f_recv.at[d], self.way(d))
+
+    def to_near(self, d, h):
+        source = self.own.at[(self.xr, self.xl)[d], h]
+        return remote(
+            source, self.near.at[d, h], self.n_send.at[d, h], self.n_recv.at[d, h], self.way(d)
+        )
+
+    def add_passed(self):
+        for h in range(2):
+            landed(self.passed.at[h], self.p_recv.at[h])
+            self.add(self.part, self.at.x, h, self.passed.at[h])
+
+    def sides_to_near(self):
+        self.side_arrived(self.xr, 1)
+        self.to_near(0, 1).start()
+        self.side_arrived(self.xl, 0)
+        self.to_near(1, 0).start()
+
+    def sides_to_far(self):
+        for h in range(2):
+            self.side_arrived(self.xf, h)
+            self.to_far(h).start()
+
+    def far_to_near(self):
+        for d, xi in ((0, self.xr), (1, self.xl)):
+            landed(self.far.at[d], self.f_recv.at[d])
+            self.add(self.own, xi, d, self.far.at[d])
+            self.to_near(d, d).start()
+
+    def arrive(self):
+        for d, h in ((0, 1), (1, 0), (0, 0), (1, 1)):
+            landed(self.near.at[d, h], self.n_recv.at[d, h])
+
+    def total(self, h, some):
+        return (
+            self.own[self.at.x, h, some, :].astype(F32)
+            + self.near[0, h, some, :].astype(F32)
+            + self.near[1, h, some, :].astype(F32)
+        )
+
+    def forward(self):
+        x = self.at.x
+        for slot, into in ((1, self.part), (0, self.own)):
+            for xi in self.pair(1):
+                self.take(slot, xi)
+            self.products(slot, 1, into)
+            if slot == 1:
+                for h in range(2):
+                    self.to_side(self.xf, h).start()
+        for xi in self.pair(0):
+            self.take(1, xi)
+        self.products(1, 0, self.part)
+        self.pass_on(0).start()
+        self.pass_on(1).start()
+        for h in range(2):
+            self.to_side(self.xf, h).wait_send()
+            self.to_side((self.xl, self.xr)[h], h).start()
+        self.sides_to_far()
+        for xi in self.pair(0):
+            self.take(0, xi)
+        self.products(0, 0, self.own)
+        self.add_passed()
+        for h in range(2):
+            self.to_side((self.xl, self.xr)[h], h).wait_send()
+            self.to_side(x, h).start()
+        self.sides_to_near()
+        self.far_to_near()
+        for h in range(2):
+            self.side_arrived(x, h)
+        self.arrive()
+
+    def backward(self, sums):
+        x = self.at.x
+
+        def first(p):
+            for xi in self.pair(p):
+                self.take(1, xi)
+            self.products(1, p, self.part)
+
+            @pl.when(p == 0)
+            def _():
+                for d in range(2):
+                    self.pass_on(d).start()
+                    self.to_side((self.xl, self.xr)[d], d).start()
+
+        loop(2, first)
+        loop(4, lambda xi: self.take(0, xi))
         loop(2, sums.tile)
 
-    def second(p):
-        if not back:
-            take(0, at.along(1 + p))
-            take(0, at.along(3 - 3 * p))
-        products(0, p, mine)
-
-        @pl.when(p == 0)
-        def _():
-            for h in range(2):
-                to_side((xl, xr)[h], h).wait_send()
-                to_side(xf, h).start()
-            for h in range(2):
-                landed(passed.at[h], p_recv.at[h])
-                add(part, at.x, h, passed.at[h])
-            side_arrived(xr, 1)
-            near_copies[0].start()
-            side_arrived(xl, 0)
-            near_copies[1].start()
-
-        if back:
+        def second(p):
+            self.products(0, p, self.own)
+
+            @pl.when(p == 0)
+            def _():
+                for h in range(2):
+                    self.to_side((self.xl, self.xr)[h], h).wait_send()
+                    self.to_side(self.xf, h).start()
+                self.add_passed()
+                self.sides_to_near()
+
             loop(2, lambda q: sums.tile(2 + 2 * p + q))
 
-    loop(2, second)
-    for h in range(2):
-        to_side(xf, h).wait_send()
-        to_side(at.x, h).start()
-    for h in range(2):
-        side_arrived(xf, h)
-        far_copies[h].start()
-    if back:
+        loop(2, second)
+        for h in range(2):
+            self.to_side(self.xf, h).wait_send()
+            self.to_side(x, h).start()
+        self.sides_to_far()
         loop(2, lambda q: sums.tile(6 + q))
         sums.merge(7)
-    for d, xi in ((0, xr), (1, xl)):
-        landed(far.at[d], f_recv.at[d])
-        add(mine, xi, d, far.at[d])
-        near_copies[2 + d].start()
-    if back:
+        self.far_to_near()
         sums.relay(1)
-    for h in range(2):
-        side_arrived(at.x, h)
-    if back:
+        for h in range(2):
+            self.side_arrived(x, h)
         sums.turn()
-    for d, h in ((0, 1), (1, 0), (0, 0), (1, 1)):
-        landed(near.at[d, h], n_recv.at[d, h])
-
-    def finish(j):
-        tile = pl.ds(pl.multiple_of(j * TILE, TILE), TILE)
-        for h in range(2):
-            total[h * HALF : (h + 1) * HALF, tile] = (
-                mine[at.x, h, :, tile].astype(F32)
-                + near[0, h, :, tile].astype(F32)
-                + near[1, h, :, tile].astype(F32)
-            )
-
-    loop(WIDTH // TILE, finish)
-    if back:
-        sums.finish()
-    for copy in pass_copies + far_copies + near_copies:
-        copy.wait_send()
-    for h in range(2):
-        to_side(at.x, h).wait_send()
-
-    loop(4, lambda i: landed(out.at[i, pl.ds(0, 15)], o_send.at[i]))
-
-
-def scatter(args, weight, back, streamed=()):
-    cols = 3 * LOCAL if back else LOCAL
-    token_shape = (2, 4, 8, 16, cols)
-    shapes = [jax.ShapeDtypeStruct((2 * HALF, WIDTH), F32)]
-    scratch = [
-        pltpu.VMEM((WIDTH, cols) if back else (LOCAL, WIDTH), BF),
+        self.arrive()
+
+    def end(self):
+        for d in range(2):
+            self.pass_on(d).wait_send()
+            self.to_far(d).wait_send()
+            for h in range(2):
+                self.to_near(d, h).wait_send()
+            self.to_side(self.at.x, d).wait_send()
+        loop(4, lambda i: landed(self.out.at[i, pl.ds(0, 15)], self.o_send.at[i]))
+
+
+def scatter_scratch(cols):
+    return [
         pltpu.VMEM((4, 16, 16, cols), BF),
         pltpu.VMEM((4, 2, HALF, WIDTH), BF),
         pltpu.VMEM((4, 2, HALF, WIDTH), BF),
@@ -756,13 +759,231 @@
         pltpu.SemaphoreType.DMA((2, 2)),
         pltpu.SemaphoreType.DMA((2,)),
         pltpu.SemaphoreType.DMA((2,)),
-        pltpu.SemaphoreType.DMA((3,)),
     ]
-    if back:
-        shapes.append(jax.ShapeDtypeStruct((4, 192, LOCAL), BF))
-        scratch += [
-            pltpu.VMEM(token_shape, BF),
+
+
+def each_rows(body):
+    def step(i):
+        inner = pl.ds(pl.multiple_of(lax.rem(i, 4) * 16, 16), 16)
+        body(lax.div(i, 4), inner, pl.ds(pl.multiple_of(i * 16, 16), 16))
+
+    loop(8, step)
+
+
+def row_factor(states):
+    return lax.rsqrt(jnp.mean(states * states, -1, keepdims=True) + 1e-06)
+
+
+def front_kernel(
+    hidden, teacher, scale, shift, gate, w_qkv, w_out,
+    kept_modded, kept_up, qkv, factors, tokens, grad_att, diff, gate_rows,
+    own, own_up, qkv_weight, out_weight, w_sem, *scratch,
+):
+    at = Place()
+    qkv_copies = load_weight(w_qkv, qkv_weight, w_sem.at[0])
+    out_copies = load_weight(w_out, out_weight, w_sem.at[1])
+    at.greet(False)
+
+    def modulate(h, inner, some):
+        states = hidden[some, :].astype(F32)
+        value = states * row_factor(states) * (1.0 + scale[...]) + shift[...]
+        own[h, inner, :] = value.astype(BF)
+
+    each_rows(modulate)
+    at.met(False)
+    ahead, middle, behind = scratch[:8], scratch[8:25], scratch[25:]
+    mix = Scatter(at, qkv, ahead[6], None, out_weight, tokens, None, None, middle)
+    end_ahead = gather_phase(
+        at, own, qkv_weight, qkv_copies, kept_modded, qkv, factors, ahead,
+        lambda: loop(2, mix.attend),
+    )
+    loop(2, lambda i: mix.attend(2 + i))
+    for copy in out_copies:
+        copy.wait()
+    mix.forward()
+    gate_rows[...] = jnp.zeros_like(gate_rows)
+
+    def compare(h, inner, some):
+        mixed = mix.total(h, inner)
+        change = hidden[some, :].astype(F32) + gate[...] * mixed - teacher[some, :].astype(F32)
+        diff[some, :] = change
+        own_up[h, inner, :] = (gate[...] * change).astype(BF)
+        both = change * mixed
+        gate_rows[...] += both[:8] + both[8:]
+
+    each_rows(compare)
+    end_behind = gather_phase(at, own_up, out_weight, [], kept_up, grad_att, None, behind)
+    end_ahead()
+    mix.end()
+    end_behind()
+    loop(4, lambda t: landed(grad_att.at[t], behind[6].at[t]))
+
+
+def front(hidden, teacher, scale, shift, gate, w_qkv, w_out):
+    kept = jax.ShapeDtypeStruct((2, 4, 2, HALF, WIDTH), BF)
+    return pl.pallas_call(
+        front_kernel,
+        out_shape=[
+            kept,
+            kept,
+            jax.ShapeDtypeStruct((4, 16, 16, 3 * LOCAL), BF),
+            jax.ShapeDtypeStruct((2, 4, 2 * HALF, HEAD_DIM), F32),
+            jax.ShapeDtypeStruct((2, 4, 8, 16, LOCAL), BF),
+            jax.ShapeDtypeStruct((4, 16, 16, LOCAL), BF),
+            jax.ShapeDtypeStruct((2 * HALF, WIDTH), F32),
+            jax.ShapeDtypeStruct((8, WIDTH), F32),
+        ],
+        in_specs=vmem(5) + anywhere(2),
+        out_specs=anywhere(2) + vmem(6),
+        scratch_shapes=[
+            pltpu.VMEM((2, HALF, WIDTH), BF),
+            pltpu.VMEM((2, HALF, WIDTH), BF),
+            pltpu.VMEM((WIDTH, 3 * LOCAL), BF),
+            pltpu.VMEM((LOCAL, WIDTH), BF),
+            pltpu.SemaphoreType.DMA((2, 3)),
+        ]
+        + gather_scratch(3 * LOCAL)
+        + scatter_scratch(LOCAL)
+        + gather_scratch(LOCAL),
+        compiler_params=pltpu.CompilerParams(
+            collective_id=0, has_side_effects=True, vmem_limit_bytes=VMEM_BYTES
+        ),
+        cost_estimate=pl.CostEstimate(
+            flops=2 * 1024 * WIDTH * 5 * LOCAL, bytes_accessed=50_000_000, transcendentals=0
+        ),
+        name="front",
+    )(hidden, teacher, scale, shift, gate, w_qkv, w_out)
+
+
+class Totals:
+    def __init__(self, at, rows, result, scratch):
+        self.at, self.rows, self.result = at, rows, result
+        (
+            self.by_head, self.by_frame, self.partial,
+            self.s1, self.r1, self.s2, self.r2, self.s3, self.r3,
+        ) = scratch
+        self.started = []
+
+    def piece(self, ref, i):
+        return ref.at[:, pl.ds(pl.multiple_of(i * LOCAL, LOCAL), LOCAL)]
+
+    def send(self, copies):
+        for copy in copies:
+            copy.start()
+        self.started += copies
+
+    def head(self, i):
+        return (self.at.fr, lax.rem(self.at.fs + i, 8))
+
+    def run(self, between):
+        fr, fs = self.at.fr, self.at.fs
+        self.send(
+            [
+                remote(
+                    self.piece(self.rows, self.head(i)[1]), self.by_head.at[fs], self.s1.at[i],
+                    self.r1, self.head(i),
+                )
+                for i in range(1, 8)
+            ]
+        )
+        self.by_head[fs] = self.piece(self.rows, fs)[...]
+        between()
+        landed(self.by_head.at[pl.ds(0, 7)], self.r1)
+        value = self.by_head[0]
+        for i in range(1, 8):
+            value = value + self.by_head[i]
+        self.partial[...] = value
+        self.by_frame[fr] = value
+        self.send(
+            [
+                remote(
+                    self.partial, self.by_frame.at[fr], self.s2.at[i], self.r2,
+                    (lax.rem(fr + i, 16), fs),
+                )
+                for i in range(1, 16)
+            ]
+        )
+        landed(self.by_frame.at[pl.ds(0, 15)], self.r2)
+        value = self.by_frame[0]
+        for i in range(1, 16):
+            value = value + self.by_frame[i]
+        here = self.piece(self.result, fs)
+        here[...] = value
+        self.send(
+            [remote(here, here, self.s3.at[i], self.r3, self.head(i)) for i in range(1, 8)]
+        )
+
+    def end(self):
+        landed(self.result.at[:, pl.ds(0, 7 * LOCAL)], self.r3)
+        for copy in self.started:
+            copy.wait_send()
+
+
+def rear_kernel(
+    hidden, diff, gate_rows, scale, qkv, grad, factors, attended, w_qkv, modded, up_all,
+    grad_hidden, w_grad, totals, weight, w_sem, tokens, dproj, scale_rows, shift_rows, rows,
+    *scratch,
+):
+    at = Place()
+    w_copies = load_weight(w_qkv, weight, w_sem)
+    sums = WeightSums(at, modded, up_all, attended, dproj, w_grad, *scratch[17:33])
+    sums.fetch(up_all, 0, 0)
+    at.greet(True)
+    at.met(True)
+    back = Scatter(at, qkv, None, grad, weight, tokens, dproj, factors, scratch[:17])
+    loop(4, back.attend)
+    loop(8, sums.out_rows)
+    for copy in w_copies:
+        copy.wait()
+    back.backward(sums)
+    scale_rows[...] = jnp.zeros_like(scale_rows)
+    shift_rows[...] = jnp.zeros_like(shift_rows)
+
+    def close(h, inner, some):
+        dmod = back.total(h, inner)
+        states = hidden[some, :].astype(F32)
+        factor = row_factor(states)
+        normed = states * factor
+        both = dmod * normed
+        scale_rows[...] += both[:8] + both[8:]
+        shift_rows[...] += dmod[:8] + dmod[8:]
+        wide = both * (1.0 + scale[...])
+        dnorm = dmod * (1.0 + scale[...])
+        value = dnorm - normed * jnp.mean(wide, -1, keepdims=True)
+        grad_hidden[some, :] = (diff[some, :] + factor * value).astype(BF)
+
+    each_rows(close)
+    rows[...] = jnp.zeros_like(rows)
+    for i, ref in enumerate((scale_rows, shift_rows, gate_rows)):
+        rows[i : i + 1, :] = jnp.sum(ref[...], 0, keepdims=True)
+    total = Totals(at, rows, totals, scratch[33:])
+    total.run(sums.finish)
+    total.end()
+    back.end()
+
+
+def rear(hidden, diff, gate_rows, scale, qkv, grad, factors, attended, w_qkv, modded, up_all):
+    cols = 3 * LOCAL
+    return pl.pallas_call(
+        rear_kernel,
+        out_shape=[
+            jax.ShapeDtypeStruct((2 * HALF, WIDTH), BF),
+            jax.ShapeDtypeStruct((4, 192, LOCAL), BF),
+            jax.ShapeDtypeStruct((8, WIDTH), F32),
+        ],
+        in_specs=vmem(8) + anywhere(3),
+        out_specs=vmem(3),
+        scratch_shapes=[
+            pltpu.VMEM((WIDTH, cols), BF),
+            pltpu.SemaphoreType.DMA((3,)),
+            pltpu.VMEM((2, 4, 8, 16, cols), BF),
             pltpu.VMEM((2, 4, 2 * HALF, cols), BF),
+            pltpu.VMEM((8, WIDTH), F32),
+            pltpu.VMEM((8, WIDTH), F32),
+            pltpu.VMEM((8, WIDTH), F32),
+        ]
+        + scatter_scratch(cols)
+        + [
             pltpu.VMEM((2, 1024, LOCAL), BF),
             pltpu.VMEM((LOCAL, 1024), BF),
             pltpu.VMEM((8, 2, 192, 4 * LOCAL), BF),
@@ -780,83 +1001,7 @@
             pltpu.SemaphoreType.DMA,
             pltpu.SemaphoreType.DMA,
         ]
-    else:
-        shapes.append(jax.ShapeDtypeStruct(token_shape, BF))
-    return pl.pallas_call(
-        functools.partial(scatter_kernel, back),
-        out_shape=shapes,
-        in_specs=vmem(len(args)) + [pl.BlockSpec(memory_space=pl.ANY)] * (1 + len(streamed)),
-        out_specs=vmem(len(shapes)),
-        scratch_shapes=scratch,
-        compiler_params=pltpu.CompilerParams(
-            collective_id=3 if back else 1,
-            has_side_effects=True,
-            vmem_limit_bytes=VMEM_BYTES,
-        ),
-        cost_estimate=pl.CostEstimate(
-            flops=2 * 1024 * WIDTH * cols, bytes_accessed=30_000_000, transcendentals=0
-        ),
-        name="scatter_back" if back else "scatter_mixed",
-    )(*args, weight, *streamed)
-
-
-def total_kernel(own, result, by_head, by_frame, partial, s1, r1, s2, r2, s3, r3):
-    fr = lax.axis_index("frame")
-    fs = lax.axis_index("fsdp")
-    barrier = pltpu.get_barrier_semaphore()
-
-    def head(i):
-        return (fr, lax.rem(fs + i, 8))
-
-    def frame(i):
-        return (lax.rem(fr + i, 16), fs)
-
-    def greet(peer):
-        pl.semaphore_signal(barrier, inc=1, device_id=peer, device_id_type=MESH)
-
-    for i in range(1, 8):
-        greet(head(i))
-    loop(15, lambda i: greet(frame(i + 1)))
-    pl.semaphore_wait(barrier, 22)
-
-    firsts = [
-        remote(own.at[head(i)[1]], by_head.at[fs], s1.at[i], r1, head(i)) for i in range(1, 8)
-    ]
-    for copy in firsts:
-        copy.start()
-    by_head[fs] = own[fs]
-    landed(by_head.at[pl.ds(0, 7)], r1)
-    value = by_head[0]
-    for i in range(1, 8):
-        value = value + by_head[i]
-    partial[...] = value
-    by_frame[fr] = value
-    seconds = [
-        remote(partial, by_frame.at[fr], s2.at[i], r2, frame(i)) for i in range(1, 16)
-    ]
-    for copy in seconds:
-        copy.start()
-    landed(by_frame.at[pl.ds(0, 15)], r2)
-    value = by_frame[0]
-    for i in range(1, 16):
-        value = value + by_frame[i]
-    result[fs] = value
-    thirds = [remote(result.at[fs], result.at[fs], s3.at[i], r3, head(i)) for i in range(1, 8)]
-    for copy in thirds:
-        copy.start()
-    landed(result.at[pl.ds(0, 7)], r3)
-    for copy in firsts + seconds + thirds:
-        copy.wait_send()
-
-
-def total_sums(rows):
-    pieces = jnp.pad(rows.reshape(3, 8, LOCAL).transpose(1, 0, 2), ((0, 0), (0, 5), (0, 0)))
-    result = pl.pallas_call(
-        total_kernel,
-        out_shape=jax.ShapeDtypeStruct((8, 8, LOCAL), F32),
-        in_specs=vmem(1),
-        out_specs=vmem(1)[0],
-        scratch_shapes=[
+        + [
             pltpu.VMEM((8, 8, LOCAL), F32),
             pltpu.VMEM((16, 8, LOCAL), F32),
             pltpu.VMEM((8, LOCAL), F32),
@@ -867,10 +1012,14 @@
             pltpu.SemaphoreType.DMA((8,)),
             pltpu.SemaphoreType.DMA,
         ],
-        compiler_params=pltpu.CompilerParams(collective_id=4, has_side_effects=True),
-        name="total_sums",
-    )(pieces)
-    return result[:, :3].transpose(1, 0, 2).reshape(3, WIDTH)
+        compiler_params=pltpu.CompilerParams(
+            collective_id=1, has_side_effects=True, vmem_limit_bytes=VMEM_BYTES
+        ),
+        cost_estimate=pl.CostEstimate(
+            flops=2 * 1024 * WIDTH * 7 * LOCAL, bytes_accessed=50_000_000, transcendentals=0
+        ),
+        name="rear",
+    )(hidden, diff, gate_rows, scale, qkv, grad, factors, attended, w_qkv, modded, up_all)
 
 
 def to_rows(block):
@@ -883,28 +1032,30 @@
 
 
 def shards(hidden_states, teacher, mod_scale, mod_shift, out_gate, w_qkv, w_out):
-    states = to_rows(hidden_states).astype(F32)
-    factor = lax.rsqrt(jnp.mean(states * states, -1, keepdims=True) + 1e-06)
-    normed = states * factor
-    modded = (normed * (1.0 + mod_scale) + mod_shift).astype(BF)
-    flat, qkv, factors = gather(modded.reshape(2, HALF, WIDTH), w_qkv, True)
-    mixed, attended = scatter([qkv], w_out, False)
-    diff = states + out_gate * mixed - to_rows(teacher).astype(F32)
-    upstream = (out_gate * diff).astype(BF)
-    up_all, grad_att = gather(upstream.reshape(2, HALF, WIDTH), w_out, False)
-    dmod, w_grad = scatter(
-        [qkv, grad_att, factors, attended.reshape(1024, LOCAL)],
+    hidden = to_rows(hidden_states)
+    scale = mod_scale.reshape(1, WIDTH)
+    modded, up_all, qkv, factors, attended, grad_att, diff, gate_rows = front(
+        hidden,
+        to_rows(teacher),
+        scale,
+        mod_shift.reshape(1, WIDTH),
+        out_gate.reshape(1, WIDTH),
         w_qkv,
-        True,
-        (flat.reshape(1024, WIDTH), up_all.reshape(1024, WIDTH)),
+        w_out,
     )
-    sums = total_sums(
-        jnp.stack([jnp.sum(dmod * normed, 0), jnp.sum(dmod, 0), jnp.sum(diff * mixed, 0)])
+    grad_hidden, w_grad, sums = rear(
+        hidden,
+        diff,
+        gate_rows,
+        scale,
+        qkv,
+        grad_att,
+        factors,
+        attended.reshape(1024, LOCAL),
+        w_qkv,
+        modded.reshape(1024, WIDTH),
+        up_all.reshape(1024, WIDTH),
     )
-    dnorm = dmod * (1.0 + mod_scale)
-    grad_hidden = (
-        diff + factor * (dnorm - normed * jnp.mean(dnorm * normed, -1, keepdims=True))
-    ).astype(BF)
     return (from_rows(grad_hidden), w_grad[:3], w_grad[3].T, sums[0], sums[1], sums[2])
 
 

time: 301 us -> 276 us (0.917)
  Pallas kernels: 281 us -> 263 us
  other arithmetic: 10.7 us -> 0 us
  local copies, waits for them, and re-layouts: 6.97 us -> 11.3 us
    pallas_call x5 -> x2, Pallas kernels: 281 us -> 263 us  [the longest x1 164 us: front(): pl.pallas_call(front_kernel, out_shape=[kept, kept, jax.ShapeDtypeStruct(...]
    reduce_sum x3 -> x0, other arithmetic: 5.76 us -> none  [the longest x1 2.26 us: shards(): jnp.sum(diff * mixed, 0)]
    reshape x0 -> x2, local copies, waits for them, and re-layouts: none -> 4.18 us  [to_rows(): block.reshape(frames, 8, 8, width).transpose(1, 0, 2, 3).reshape(-1, width)]
    convert_element_type x5 -> x0, other arithmetic: 4.13 us -> none  [the longest x1 1.28 us: shards(): diff = states + out_gate * mixed - to_rows(teacher).astype(F32)]
where the time goes in v4:
time: 276 us; the launch traced here: 275 us
  Pallas kernels  263 us (95%)
  local copies, waits for them, and re-layouts  11.3 us (4%)
    pallas_call x1, Pallas kernels, front(): pl.pallas_call(front_kernel, out_shape=[kept, kept, jax.ShapeDtypeStruct(...  164 us
    pallas_call x1, Pallas kernels, rear(): pl.pallas_call(rear_kernel, out_shape=[jax.ShapeDtypeStruct((2 * HALF, WI...  99.2 us

profile of v4, /device:TPU:1, one launch (start us, length us, event | category | flops | bytes accessed | tf_op | source)
XLA Modules:
  0.0 275.3 jit_solution(12516860258655026033)
XLA Ops:
  0.6 2.1 copy.13
  2.7 2.1 copy.14
  4.8 164.2 %front.1 = (bf16[2,4,2,64,3072]{4,3,2,1,0:T(8,128)(2,1)}, bf16[2,4,2,64,3072]{4,3,2,1,0:T(8,128)(2,1)}, bf16[4,16,16,1152]{3,2,1,0:T(8,128)(2,1)}, f32[2,4,128,1...) custom-call(bf16[128,3072]{1,0:T(8,128)(2,1)} %bitcast.30, ...), custom_call_target="tpu_custom_call" | custom-call | flops 12079595520 | bytes 50000000 | tf_op jit(solution)/shard_map/front/pallas_call | solution.py:824
  169.0 99.2 %rear.1 = (bf16[128,3072]{1,0:T(8,128)(2,1)}, bf16[4,192,384]{2,1,0:T(8,128)(2,1)}, f32[8,3072]{1,0:T(8,128)}) custom-call(bf16[128,3072]{1,0:T(8,128)(2,1)} %bitcast.31, f32[128,3072]{1,0:T(8,128)} %get-tuple-element.17.diff, f32[8,3072]{1,0:T(8,128)} %get-tuple-element.18.gate_rows, f32[1,3072]{1,0:T(1,128)} %bitcast.40, ...), custom_call_target="tpu_custom_call" | custom-call | flops 16911433728 | bytes 50000000 | tf_op jit(solution)/shard_map/rear/pallas_call | solution.py:967
  268.2 2.1 copy.17
  270.3 1.7 fusion
  271.9 1.6 slice_bitcast_fusion
  273.5 1.8 slice.15

commit v5 on v4

--- a/solution.py
+++ b/solution.py
@@ -30,10 +30,16 @@
         self.core = lax.rem(fr, 2)
         self.group = lax.div(fr, 2)
         other = fs + 1 - 2 * self.lo
-        hi = lax.rem(self.group, 2)
+        self.hi = lax.rem(self.group, 2)
+        self.z = lax.div(self.group, 2)
         self.right = (fr, lax.rem(fs + 2, 8))
         self.left = (fr, lax.rem(fs + 6, 8))
-        self.side = ((fr, other), (fr + 2 - 4 * hi, other))
+        self.side = tuple((self.frame(self.z, h, self.core), other) for h in range(2))
+        self.across = (fr + 2 - 4 * self.hi, other)
+        self.beside = (fr, other)
+
+    def frame(self, z, hi, core):
+        return 4 * z + 2 * hi + core
 
     def along(self, off):
         return lax.rem(self.x + off, 4)
@@ -44,12 +50,12 @@
         def signal(peer):
             pl.semaphore_signal(barrier, inc=1, device_id=peer, device_id_type=MESH)
 
-        signal(self.side[1])
+        signal(self.across)
         if heads:
             for step in range(1, 8):
                 signal((self.fr, lax.rem(self.fs + step, 8)))
         else:
-            for peer in (self.right, self.left, self.side[0]):
+            for peer in (self.right, self.left, self.beside):
                 signal(peer)
         loop(15, lambda i: signal((lax.rem(self.fr + i + 1, 16), self.fs)))
 
@@ -108,7 +114,9 @@
         return remote(src, full.at[slot, xi, h], x_send.at[n], recv.at[slot, xi, h], at.left)
 
     def to_side(src, xi, h, n):
-        return remote(src, full.at[1, xi, h], y_send.at[n], recv.at[1, xi, h], at.side[h])
+        return remote(
+            src, full.at[1, xi, at.hi], y_send.at[n], recv.at[1, xi, at.hi], at.side[h]
+        )
 
     xl, xr, xf = at.along(3), at.along(1), at.along(2)
     first = [
@@ -124,9 +132,6 @@
         to_right(0, full.at[0, xl, 0], xl, 0, 2),
         to_left(0, full.at[0, xr, 1], xr, 1, 3),
     ]
-    if not project:
-        second.append(to_side(full.at[0, xl, 0], xl, 0, 2))
-        second.append(to_side(full.at[0, xr, 1], xr, 1, 3))
     third = [
         to_right(0, own.at[1], at.x, 1, 4),
         to_side(full.at[0, xf, 0], xf, 0, 4),
@@ -140,6 +145,8 @@
     if project:
         fourth.append(to_right(1, full.at[1, at.x, 0], at.x, 0, 8))
         fourth.append(to_left(1, full.at[1, at.x, 1], at.x, 1, 9))
+    early_sides = [to_side(full.at[0, (xl, xr)[h], h], (xl, xr)[h], h, 2) for h in range(2)]
+    late_sides = [to_side(full.at[0, (xl, xr)[h], 1 - h], (xl, xr)[h], 1 - h, 3) for h in range(2)]
     for copy in w_copies:
         copy.wait()
 
@@ -150,11 +157,13 @@
         @pl.when(k == 1)
         def _():
             arrived(0, xl, 0)
-            for copy in second[0::2]:
-                copy.start()
+            second[0].start()
+            if not project:
+                pl.when(at.hi == 0)(lambda: early_sides[0].start())
             arrived(0, xr, 1)
-            for copy in second[1::2]:
-                copy.start()
+            second[1].start()
+            if not project:
+                pl.when(at.hi == 1)(lambda: early_sides[1].start())
             arrived(1, at.x, 0)
             arrived(1, at.x, 1)
 
@@ -178,12 +187,16 @@
             arrived(0, xl, 1)
             for copy in fourth[0::2]:
                 copy.start()
+            if not project:
+                pl.when(at.hi == 0)(lambda: late_sides[0].start())
 
         @pl.when(i == 2)
         def _():
             arrived(0, xr, 0)
             for copy in fourth[1::2]:
                 copy.start()
+            if not project:
+                pl.when(at.hi == 1)(lambda: late_sides[1].start())
 
         if between is not None:
             pl.when(i == 4)(between)
@@ -208,7 +221,7 @@
                     factor = lax.rsqrt(jnp.mean(block * block, -1, keepdims=True) + 1e-06)
                     kept = jnp.where(lane == j, factor, kept)
                     block = block * factor
-                out[k, :, :, j * HEAD_DIM : (j + 1) * HEAD_DIM] = block.astype(BF).reshape(
+                out[pl.ds(8 * k, 8), :, j * HEAD_DIM : (j + 1) * HEAD_DIM] = block.astype(BF).reshape(
                     8, 16, HEAD_DIM
                 )
             factors[slot, xi] = kept
@@ -216,14 +229,16 @@
             both = lax.dot_general(
                 tokens, weight[...], (((1,), (1,)), ((), ())), preferred_element_type=F32
             )
-            out[k] = both.astype(BF).reshape(8, 16, LOCAL)
+            out[pl.ds(8 * k, 8)] = both.astype(BF).reshape(8, 16, LOCAL)
         to_core = lax.rem(xi, 2)
         to_slot = 2 * lax.div(xi, 2) + lax.rem(at.lo + slot, 2)
 
-        def give(g):
-            target = 2 * g + to_core
-            src = out.at[k, g]
-            dst = sent_to.at[to_slot, at.fr]
+        def give(b):
+            z, upper = lax.rem(b, 4), lax.div(b, 4)
+            target = at.frame(z, (1 - slot) * upper + slot * at.hi, to_core)
+            origin = at.frame(at.z, (1 - slot) * at.hi + slot * upper, at.core)
+            src = out.at[8 * k + b]
+            dst = sent_to.at[to_slot, origin]
 
             @pl.when(target == at.fr)
             def _():
@@ -231,26 +246,24 @@
 
             @pl.when(target != at.fr)
             def _():
-                remote(src, dst, o_send.at[g], o_recv.at[to_slot], (target, at.fs)).start()
+                remote(src, dst, o_send, o_recv.at[to_slot], (target, at.fs)).start()
 
         loop(8, give)
 
     loop(2, early)
     loop(6, late)
-
-    def drain(g):
-        @pl.when(g == at.group)
-        def _():
-            landed(out.at[pl.ds(0, 4), g], o_send.at[g])
-
-        @pl.when(g != at.group)
-        def _():
-            landed(out.at[:, g], o_send.at[g])
 
     def end():
         for copy in first + second + third + fourth:
             copy.wait_send()
-        loop(8, drain)
+        for h in range(0 if project else 2):
+
+            @pl.when(at.hi == h)
+            def _(h=h):
+                early_sides[h].wait_send()
+                late_sides[h].wait_send()
+
+        landed(out.at[pl.ds(0, 58)], o_send)
         pltpu.make_async_copy(full, kept_all, keep_sem).wait()
 
     return end
@@ -259,11 +272,11 @@
 def gather_scratch(cols):
     return [
         pltpu.VMEM((2, 4, 2, HALF, WIDTH), BF),
-        pltpu.VMEM((8, 8, 16, cols), BF),
+        pltpu.VMEM((64, 16, cols), BF),
         pltpu.SemaphoreType.DMA((10,)),
         pltpu.SemaphoreType.DMA((6,)),
         pltpu.SemaphoreType.DMA((2, 4, 2)),
-        pltpu.SemaphoreType.DMA((8,)),
+        pltpu.SemaphoreType.DMA,
         pltpu.SemaphoreType.DMA((4,)),
         pltpu.SemaphoreType.DMA,
     ]
@@ -471,8 +484,9 @@
                 there = pl.ds(pl.multiple_of(half * 96 + i * 48, 16), 48)
                 value = self.both(1, half, some) + self.last[there, :].astype(F32)
                 value = value.astype(BF)
-                for c in range(4):
-                    self.result[c, there, :] = value[:, c * LOCAL : (c + 1) * LOCAL]
+                for c in range(3):
+                    self.result[0][c, there, :] = value[:, c * LOCAL : (c + 1) * LOCAL]
+                self.result[1][there, :] = value[:, 3 * LOCAL :]
 
             loop(2, end)
         for d in range(2):
@@ -542,17 +556,20 @@
         xi = 2 * xh + at.core
 
         def give(f):
+            upper = lax.rem(lax.div(f, 2), 2)
+            target = f + 2 * slot * (at.hi - upper)
+            piece = 4 * ((1 - slot) * at.hi + slot * upper) + at.z
             src = self.out.at[i, f]
-            dst = self.tokens.at[slot, xi, at.group]
-
-            @pl.when(f == at.fr)
+            dst = self.tokens.at[slot, xi, piece]
+
+            @pl.when(target == at.fr)
             def _():
                 pltpu.make_async_copy(src, dst, self.o_recv.at[slot, xi]).start()
 
-            @pl.when(f != at.fr)
+            @pl.when(target != at.fr)
             def _():
                 remote(
-                    src, dst, self.o_send.at[i], self.o_recv.at[slot, xi], (f, at.fs)
+                    src, dst, self.o_send.at[i], self.o_recv.at[slot, xi], (target, at.fs)
                 ).start()
 
         loop(16, give)
@@ -596,8 +613,8 @@
 
     def to_side(self, xi, h):
         return remote(
-            self.part.at[xi, h], self.from_side.at[xi, h], self.y_send.at[xi, h],
-            self.y_recv.at[xi, h], self.at.side[h],
+            self.part.at[xi, h], self.from_side.at[xi, self.at.hi], self.y_send.at[xi, h],
+            self.y_recv.at[xi, self.at.hi], self.at.side[h],
         )
 
     def side_arrived(self, xi, h):
@@ -627,9 +644,9 @@
             self.add(self.part, self.at.x, h, self.passed.at[h])
 
     def sides_to_near(self):
-        self.side_arrived(self.xr, 1)
+        for h in range(2):
+            self.side_arrived(self.at.along(3 - 2 * self.at.hi), h)
         self.to_near(0, 1).start()
-        self.side_arrived(self.xl, 0)
         self.to_near(1, 0).start()
 
     def sides_to_far(self):
@@ -737,7 +754,9 @@
             for h in range(2):
                 self.to_near(d, h).wait_send()
             self.to_side(self.at.x, d).wait_send()
-        loop(4, lambda i: landed(self.out.at[i, pl.ds(0, 15)], self.o_send.at[i]))
+        for i in range(4):
+            other = (i < 2) == self.back
+            landed(self.out.at[i, pl.ds(0, 14 if other else 15)], self.o_send.at[i])
 
 
 def scatter_scratch(cols):
@@ -763,11 +782,17 @@
 
 
 def each_rows(body):
-    def step(i):
-        inner = pl.ds(pl.multiple_of(lax.rem(i, 4) * 16, 16), 16)
-        body(lax.div(i, 4), inner, pl.ds(pl.multiple_of(i * 16, 16), 16))
-
-    loop(8, step)
+    loop(4, lambda j: body(j))
+
+
+def pieces(ref, j):
+    first, second = (ref[f, pl.ds(pl.multiple_of(16 * j, 16), 16), :].astype(F32) for f in range(2))
+    return [jnp.concatenate([first[i : i + 8], second[i : i + 8]]) for i in (0, 8)]
+
+
+def place_of(j, n):
+    inner = pl.ds(pl.multiple_of(lax.rem(j, 2) * 32 + 16 * n, 16), 16)
+    return lax.div(j, 2), inner, pl.ds(pl.multiple_of(j * 32 + 16 * n, 16), 16)
 
 
 def row_factor(states):
@@ -784,10 +809,11 @@
     out_copies = load_weight(w_out, out_weight, w_sem.at[1])
     at.greet(False)
 
-    def modulate(h, inner, some):
-        states = hidden[some, :].astype(F32)
-        value = states * row_factor(states) * (1.0 + scale[...]) + shift[...]
-        own[h, inner, :] = value.astype(BF)
+    def modulate(j):
+        for n, states in enumerate(pieces(hidden, j)):
+            h, inner, _ = place_of(j, n)
+            value = states * row_factor(states) * (1.0 + scale[...]) + shift[...]
+            own[h, inner, :] = value.astype(BF)
 
     each_rows(modulate)
     at.met(False)
@@ -803,13 +829,15 @@
     mix.forward()
     gate_rows[...] = jnp.zeros_like(gate_rows)
 
-    def compare(h, inner, some):
-        mixed = mix.total(h, inner)
-        change = hidden[some, :].astype(F32) + gate[...] * mixed - teacher[some, :].astype(F32)
-        diff[some, :] = change
-        own_up[h, inner, :] = (gate[...] * change).astype(BF)
-        both = change * mixed
-        gate_rows[...] += both[:8] + both[8:]
+    def compare(j):
+        for n, (states, target) in enumerate(zip(pieces(hidden, j), pieces(teacher, j))):
+            h, inner, some = place_of(j, n)
+            mixed = mix.total(h, inner)
+            change = states + gate[...] * mixed - target
+            diff[some, :] = change
+            own_up[h, inner, :] = (gate[...] * change).astype(BF)
+            both = change * mixed
+            gate_rows[...] += both[:8] + both[8:]
 
     each_rows(compare)
     end_behind = gather_phase(at, own_up, out_weight, [], kept_up, grad_att, None, behind)
@@ -875,7 +903,7 @@
     def head(self, i):
         return (self.at.fr, lax.rem(self.at.fs + i, 8))
 
-    def run(self, between):
+    def run(self, between, later):
         fr, fs = self.at.fr, self.at.fs
         self.send(
             [
@@ -903,6 +931,7 @@
                 for i in range(1, 16)
             ]
         )
+        later()
         landed(self.by_frame.at[pl.ds(0, 15)], self.r2)
         value = self.by_frame[0]
         for i in range(1, 16):
@@ -921,12 +950,12 @@
 
 def rear_kernel(
     hidden, diff, gate_rows, scale, qkv, grad, factors, attended, w_qkv, modded, up_all,
-    grad_hidden, w_grad, totals, weight, w_sem, tokens, dproj, scale_rows, shift_rows, rows,
+    grad_hidden, qkv_grad, out_grad, totals, weight, w_sem, tokens, dproj, scale_rows, shift_rows, rows,
     *scratch,
 ):
     at = Place()
     w_copies = load_weight(w_qkv, weight, w_sem)
-    sums = WeightSums(at, modded, up_all, attended, dproj, w_grad, *scratch[17:33])
+    sums = WeightSums(at, modded, up_all, attended, dproj, (qkv_grad, out_grad), *scratch[17:33])
     sums.fetch(up_all, 0, 0)
     at.greet(True)
     at.met(True)
@@ -939,25 +968,33 @@
     scale_rows[...] = jnp.zeros_like(scale_rows)
     shift_rows[...] = jnp.zeros_like(shift_rows)
 
-    def close(h, inner, some):
-        dmod = back.total(h, inner)
-        states = hidden[some, :].astype(F32)
-        factor = row_factor(states)
-        normed = states * factor
-        both = dmod * normed
-        scale_rows[...] += both[:8] + both[8:]
-        shift_rows[...] += dmod[:8] + dmod[8:]
-        wide = both * (1.0 + scale[...])
-        dnorm = dmod * (1.0 + scale[...])
-        value = dnorm - normed * jnp.mean(wide, -1, keepdims=True)
-        grad_hidden[some, :] = (diff[some, :] + factor * value).astype(BF)
-
-    each_rows(close)
+    def add_up(j):
+        for n, states in enumerate(pieces(hidden, j)):
+            h, inner, _ = place_of(j, n)
+            dmod = back.total(h, inner)
+            both = dmod * (states * row_factor(states))
+            scale_rows[...] += both[:8] + both[8:]
+            shift_rows[...] += dmod[:8] + dmod[8:]
+
+    def close(j):
+        done = []
+        for n, states in enumerate(pieces(hidden, j)):
+            h, inner, some = place_of(j, n)
+            factor = row_factor(states)
+            normed = states * factor
+            dnorm = back.total(h, inner) * (1.0 + scale[...])
+            value = dnorm - normed * jnp.mean(dnorm * normed, -1, keepdims=True)
+            done.append(diff[some, :] + factor * value)
+        for f in range(2):
+            both = jnp.concatenate([value[8 * f : 8 * f + 8] for value in done])
+            grad_hidden[f, pl.ds(pl.multiple_of(16 * j, 16), 16), :] = both.astype(BF)
+
+    each_rows(add_up)
     rows[...] = jnp.zeros_like(rows)
     for i, ref in enumerate((scale_rows, shift_rows, gate_rows)):
         rows[i : i + 1, :] = jnp.sum(ref[...], 0, keepdims=True)
     total = Totals(at, rows, totals, scratch[33:])
-    total.run(sums.finish)
+    total.run(lambda: each_rows(close), sums.finish)
     total.end()
     back.end()
 
@@ -967,12 +1004,13 @@
     return pl.pallas_call(
         rear_kernel,
         out_shape=[
-            jax.ShapeDtypeStruct((2 * HALF, WIDTH), BF),
-            jax.ShapeDtypeStruct((4, 192, LOCAL), BF),
+            jax.ShapeDtypeStruct((2, HALF, WIDTH), BF),
+            jax.ShapeDtypeStruct((3, 192, LOCAL), BF),
+            jax.ShapeDtypeStruct((192, LOCAL), BF),
             jax.ShapeDtypeStruct((8, WIDTH), F32),
         ],
         in_specs=vmem(8) + anywhere(3),
-        out_specs=vmem(3),
+        out_specs=vmem(4),
         scratch_shapes=[
             pltpu.VMEM((WIDTH, cols), BF),
             pltpu.SemaphoreType.DMA((3,)),
@@ -1022,29 +1060,46 @@
     )(hidden, diff, gate_rows, scale, qkv, grad, factors, attended, w_qkv, modded, up_all)
 
 
-def to_rows(block):
-    frames, patches, width = block.shape
-    return block.reshape(frames, 8, 8, width).transpose(1, 0, 2, 3).reshape(-1, width)
-
-
-def from_rows(rows):
-    return rows.reshape(8, 2, 8, -1).transpose(1, 0, 2, 3).reshape(2, 64, -1)
+def hand_over_kernel(hidden, qkv, out, totals, to_hidden, to_qkv, to_out, *to_rows):
+    to_hidden[...] = hidden[...]
+    to_qkv[...] = qkv[...]
+    to_out[...] = out[...].astype(F32).T.astype(BF)
+    for i, ref in enumerate(to_rows):
+        ref[...] = totals[i]
+
+
+def hand_over(hidden, qkv, out, totals):
+    row = jax.ShapeDtypeStruct((WIDTH,), F32)
+    return pl.pallas_call(
+        hand_over_kernel,
+        out_shape=[
+            jax.ShapeDtypeStruct(hidden.shape, BF),
+            jax.ShapeDtypeStruct(qkv.shape, BF),
+            jax.ShapeDtypeStruct(out.shape[::-1], BF),
+            row,
+            row,
+            row,
+        ],
+        in_specs=vmem(4),
+        out_specs=vmem(6),
+        compiler_params=pltpu.CompilerParams(vmem_limit_bytes=VMEM_BYTES),
+        name="hand_over",
+    )(hidden, qkv, out, totals)
 
 
 def shards(hidden_states, teacher, mod_scale, mod_shift, out_gate, w_qkv, w_out):
-    hidden = to_rows(hidden_states)
     scale = mod_scale.reshape(1, WIDTH)
     modded, up_all, qkv, factors, attended, grad_att, diff, gate_rows = front(
-        hidden,
-        to_rows(teacher),
+        hidden_states,
+        teacher,
         scale,
         mod_shift.reshape(1, WIDTH),
         out_gate.reshape(1, WIDTH),
         w_qkv,
         w_out,
     )
-    grad_hidden, w_grad, sums = rear(
-        hidden,
+    results = rear(
+        hidden_states,
         diff,
         gate_rows,
         scale,
@@ -1056,7 +1111,7 @@
         modded.reshape(1024, WIDTH),
         up_all.reshape(1024, WIDTH),
     )
-    return (from_rows(grad_hidden), w_grad[:3], w_grad[3].T, sums[0], sums[1], sums[2])
+    return hand_over(*results)
 
 
 def solution(mesh):

time: 276 us -> 264 us (0.957)
  local copies, waits for them, and re-layouts: 11.3 us -> 1.71 us
    reshape x2 -> x0, local copies, waits for them, and re-layouts: 4.18 us -> none  [to_rows(): block.reshape(frames, 8, 8, width).transpose(1, 0, 2, 3).reshape(-1, width)]
    transpose x2 -> x0, local copies, waits for them, and re-layouts: 3.65 us -> none  [the longest x1 2.06 us: from_rows(): return rows.reshape(8, 2, 8, -1).transpose(1, 0, 2, 3).reshape(2, 64, -1)]
    slice x2 -> x0, local copies, waits for them, and re-layouts: 3.49 us -> none  [the longest x1 1.82 us: shards(): w_grad[:3]]
    pallas_call x1 -> x2, Pallas kernels: 99.2 us -> 99.7 us  [the longest x1 97.2 us: rear(): pl.pallas_call(rear_kernel, out_shape=[jax.ShapeDtypeStruct((2, HALF, WID...]
where the time goes in v5:
time: 264 us
  Pallas kernels  261 us (99%)
    pallas_call x1, Pallas kernels, front(): pl.pallas_call(front_kernel, out_shape=[kept, kept, jax.ShapeDtypeStruct(...  161 us
    pallas_call x1, Pallas kernels, rear(): pl.pallas_call(rear_kernel, out_shape=[jax.ShapeDtypeStruct((2, HALF, WID...  97.2 us

profile of v5, /device:TPU:1, one launch (start us, length us, event | category | flops | bytes accessed | tf_op | source)
XLA Modules:
  0.0 263.5 jit_solution(1729499343419318160)
XLA Ops:
  0.6 161.5 %front.1 = (bf16[2,4,2,64,3072]{4,3,2,1,0:T(8,128)(2,1)}, bf16[2,4,2,64,3072]{4,3,2,1,0:T(8,128)(2,1)}, bf16[4,16,16,1152]{3,2,1,0:T(8,128)(2,1)}, f32[2,4,128,1...) custom-call(bf16[2,64,3072]{2,1,0:T(8,128)(2,1)} %hidden.3, ...), custom_call_target="tpu_custom_call" | custom-call | flops 12079595520 | bytes 50000000 | tf_op jit(solution)/shard_map/front/pallas_call | solution.py:852
  162.1 97.2 %rear.1 = (bf16[2,64,3072]{2,1,0:T(8,128)(2,1)}, bf16[3,192,384]{2,1,0:T(8,128)(2,1)}, bf16[192,384]{1,0:T(8,128)(2,1)}, f32[8,3072]{1,0:T(8,128)}) custom-call(bf16[2,64,3072]{2,1,0:T(8,128)(2,1)} %hidden.3, f32[128,3072]{1,0:T(8,128)} %get-tuple-element.18.diff, f32[8,3072]{1,0:T(8,128)} %get-tuple-element.19.gate_rows, f32[1,3072]{1,0:T(1,128)} %bitcast.9, ...), custom_call_target="tpu_custom_call" | custom-call | flops 16911433728 | bytes 50000000 | tf_op jit(solution)/shard_map/rear/pallas_call | solution.py:1004
  259.4 2.5 hand_over.1
  261.8 1.7 copy.13

commit v6 on v5

--- a/solution.py
+++ b/solution.py
@@ -801,8 +801,8 @@
 
 def front_kernel(
     hidden, teacher, scale, shift, gate, w_qkv, w_out,
-    kept_modded, kept_up, qkv, factors, tokens, grad_att, diff, gate_rows,
-    own, own_up, qkv_weight, out_weight, w_sem, *scratch,
+    kept_modded, kept_up, qkv_hbm, factors_hbm, tokens_hbm, diff_hbm, grad_att, gate_rows,
+    qkv, factors, tokens, diff, out_sem, own, own_up, qkv_weight, out_weight, w_sem, *scratch,
 ):
     at = Place()
     qkv_copies = load_weight(w_qkv, qkv_weight, w_sem.at[0])
@@ -840,7 +840,17 @@
             gate_rows[...] += both[:8] + both[8:]
 
     each_rows(compare)
+    leaving = [
+        pltpu.make_async_copy(here, there, out_sem.at[i])
+        for i, (here, there) in enumerate(
+            ((qkv, qkv_hbm), (factors, factors_hbm), (tokens, tokens_hbm), (diff, diff_hbm))
+        )
+    ]
+    for copy in leaving:
+        copy.start()
     end_behind = gather_phase(at, own_up, out_weight, [], kept_up, grad_att, None, behind)
+    for copy in leaving:
+        copy.wait()
     end_ahead()
     mix.end()
     end_behind()
@@ -857,13 +867,18 @@
             jax.ShapeDtypeStruct((4, 16, 16, 3 * LOCAL), BF),
             jax.ShapeDtypeStruct((2, 4, 2 * HALF, HEAD_DIM), F32),
             jax.ShapeDtypeStruct((2, 4, 8, 16, LOCAL), BF),
+            jax.ShapeDtypeStruct((2 * HALF, WIDTH), F32),
             jax.ShapeDtypeStruct((4, 16, 16, LOCAL), BF),
-            jax.ShapeDtypeStruct((2 * HALF, WIDTH), F32),
             jax.ShapeDtypeStruct((8, WIDTH), F32),
         ],
         in_specs=vmem(5) + anywhere(2),
-        out_specs=anywhere(2) + vmem(6),
+        out_specs=anywhere(6) + vmem(2),
         scratch_shapes=[
+            pltpu.VMEM((4, 16, 16, 3 * LOCAL), BF),
+            pltpu.VMEM((2, 4, 2 * HALF, HEAD_DIM), F32),
+            pltpu.VMEM((2, 4, 8, 16, LOCAL), BF),
+            pltpu.VMEM((2 * HALF, WIDTH), F32),
+            pltpu.SemaphoreType.DMA((4,)),
             pltpu.VMEM((2, HALF, WIDTH), BF),
             pltpu.VMEM((2, HALF, WIDTH), BF),
             pltpu.VMEM((WIDTH, 3 * LOCAL), BF),
@@ -949,18 +964,34 @@
 
 
 def rear_kernel(
-    hidden, diff, gate_rows, scale, qkv, grad, factors, attended, w_qkv, modded, up_all,
-    grad_hidden, qkv_grad, out_grad, totals, weight, w_sem, tokens, dproj, scale_rows, shift_rows, rows,
+    gate_rows, scale, qkv, grad, hidden_hbm, diff_hbm, factors_hbm, attended_hbm, w_qkv, modded,
+    up_all, grad_hidden, qkv_grad, out_grad, totals, hidden, diff, factors, attended, in_sem, weight,
+    w_sem, tokens, dproj, scale_rows, shift_rows, rows,
     *scratch,
 ):
     at = Place()
+    late = [
+        pltpu.make_async_copy(source, here, in_sem.at[i])
+        for i, (source, here) in enumerate(
+            (
+                (attended_hbm, attended),
+                (factors_hbm, factors),
+                (hidden_hbm, hidden),
+                (diff_hbm, diff),
+            )
+        )
+    ]
     w_copies = load_weight(w_qkv, weight, w_sem)
+    for copy in late:
+        copy.start()
     sums = WeightSums(at, modded, up_all, attended, dproj, (qkv_grad, out_grad), *scratch[17:33])
     sums.fetch(up_all, 0, 0)
     at.greet(True)
     at.met(True)
     back = Scatter(at, qkv, None, grad, weight, tokens, dproj, factors, scratch[:17])
     loop(4, back.attend)
+    for copy in late:
+        copy.wait()
     loop(8, sums.out_rows)
     for copy in w_copies:
         copy.wait()
@@ -1009,9 +1040,14 @@
             jax.ShapeDtypeStruct((192, LOCAL), BF),
             jax.ShapeDtypeStruct((8, WIDTH), F32),
         ],
-        in_specs=vmem(8) + anywhere(3),
+        in_specs=vmem(4) + anywhere(7),
         out_specs=vmem(4),
         scratch_shapes=[
+            pltpu.VMEM((2, HALF, WIDTH), BF),
+            pltpu.VMEM((2 * HALF, WIDTH), F32),
+            pltpu.VMEM((2, 4, 2 * HALF, HEAD_DIM), F32),
+            pltpu.VMEM((1024, LOCAL), BF),
+            pltpu.SemaphoreType.DMA((4,)),
             pltpu.VMEM((WIDTH, cols), BF),
             pltpu.SemaphoreType.DMA((3,)),
             pltpu.VMEM((2, 4, 8, 16, cols), BF),
@@ -1057,13 +1093,13 @@
             flops=2 * 1024 * WIDTH * 7 * LOCAL, bytes_accessed=50_000_000, transcendentals=0
         ),
         name="rear",
-    )(hidden, diff, gate_rows, scale, qkv, grad, factors, attended, w_qkv, modded, up_all)
+    )(gate_rows, scale, qkv, grad, hidden, diff, factors, attended, w_qkv, modded, up_all)
 
 
 def hand_over_kernel(hidden, qkv, out, totals, to_hidden, to_qkv, to_out, *to_rows):
     to_hidden[...] = hidden[...]
     to_qkv[...] = qkv[...]
-    to_out[...] = out[...].astype(F32).T.astype(BF)
+    to_out[...] = out[...]
     for i, ref in enumerate(to_rows):
         ref[...] = totals[i]
 
@@ -1075,7 +1111,7 @@
         out_shape=[
             jax.ShapeDtypeStruct(hidden.shape, BF),
             jax.ShapeDtypeStruct(qkv.shape, BF),
-            jax.ShapeDtypeStruct(out.shape[::-1], BF),
+            jax.ShapeDtypeStruct(out.shape, BF),
             row,
             row,
             row,
@@ -1089,7 +1125,7 @@
 
 def shards(hidden_states, teacher, mod_scale, mod_shift, out_gate, w_qkv, w_out):
     scale = mod_scale.reshape(1, WIDTH)
-    modded, up_all, qkv, factors, attended, grad_att, diff, gate_rows = front(
+    modded, up_all, qkv, factors, attended, diff, grad_att, gate_rows = front(
         hidden_states,
         teacher,
         scale,
@@ -1111,7 +1147,8 @@
         modded.reshape(1024, WIDTH),
         up_all.reshape(1024, WIDTH),
     )
-    return hand_over(*results)
+    grad_hidden, qkv_grad, out_grad, *sums = hand_over(*results)
+    return (grad_hidden, qkv_grad, out_grad.T, *sums)
 
 
 def solution(mesh):

time: 264 us -> 260 us (0.985)
  no operation moved by 1% of the time
where the time goes in v6:
time: 260 us; the launch traced here: 259 us
  Pallas kernels  259 us (100%)
    pallas_call x1, Pallas kernels, front(): pl.pallas_call(front_kernel, out_shape=[kept, kept, jax.ShapeDtypeStruct(...  160 us
    pallas_call x1, Pallas kernels, rear(): pl.pallas_call(rear_kernel, out_shape=[jax.ShapeDtypeStruct((2, HALF, WID...  96.5 us

profile of v6, /device:TPU:1, one launch (start us, length us, event | category | flops | bytes accessed | tf_op | source)
XLA Modules:
  0.0 259.4 jit_solution(15996835032881713820)
XLA Ops:
  0.6 159.8 %front.1 = (bf16[2,4,2,64,3072]{4,3,2,1,0:T(8,128)(2,1)}, bf16[2,4,2,64,3072]{4,3,2,1,0:T(8,128)(2,1)}, bf16[4,16,16,1152]{3,2,1,0:T(8,128)(2,1)}, f32[2,4,128,1...) custom-call(bf16[2,64,3072]{2,1,0:T(8,128)(2,1)} %hidden_hbm.1, ...), custom_call_target="tpu_custom_call" | custom-call | flops 12079595520 | bytes 50000000 | tf_op jit(solution)/shard_map/front/pallas_call | solution.py:862
  160.5 96.5 %rear.1 = (bf16[2,64,3072]{2,1,0:T(8,128)(2,1)}, bf16[3,192,384]{2,1,0:T(8,128)(2,1)}, bf16[192,384]{1,0:T(8,128)(2,1)}, f32[8,3072]{1,0:T(8,128)}) custom-call(f32[8,3072]{1,0:T(8,128)} %get-tuple-element.24.gate_rows, f32[1,3072]{1,0:T(1,128)} %bitcast.11, bf16[4,16,16,1152]{3,2,1,0:T(8,128)(2,1)} %get-tuple-element.25.qkv, ...), custom_call_target="tpu_custom_call" | custom-call | flops 16911433728 | bytes 50000000 | tf_op jit(solution)/shard_map/rear/pallas_call | solution.py:1035
  256.9 2.4 hand_over.1

commit v7 on v6

--- a/solution.py
+++ b/solution.py
@@ -664,11 +664,11 @@
         for d, h in ((0, 1), (1, 0), (0, 0), (1, 1)):
             landed(self.near.at[d, h], self.n_recv.at[d, h])
 
-    def total(self, h, some):
+    def total(self, h, some, cols=slice(None)):
         return (
-            self.own[self.at.x, h, some, :].astype(F32)
-            + self.near[0, h, some, :].astype(F32)
-            + self.near[1, h, some, :].astype(F32)
+            self.own[self.at.x, h, some, cols].astype(F32)
+            + self.near[0, h, some, cols].astype(F32)
+            + self.near[1, h, some, cols].astype(F32)
         )
 
     def forward(self):
@@ -785,8 +785,8 @@
     loop(4, lambda j: body(j))
 
 
-def pieces(ref, j):
-    first, second = (ref[f, pl.ds(pl.multiple_of(16 * j, 16), 16), :].astype(F32) for f in range(2))
+def pieces(ref, j, cols=slice(None)):
+    first, second = (ref[f, pl.ds(pl.multiple_of(16 * j, 16), 16), cols].astype(F32) for f in range(2))
     return [jnp.concatenate([first[i : i + 8], second[i : i + 8]]) for i in (0, 8)]
 
 
@@ -830,14 +830,19 @@
     gate_rows[...] = jnp.zeros_like(gate_rows)
 
     def compare(j):
-        for n, (states, target) in enumerate(zip(pieces(hidden, j), pieces(teacher, j))):
-            h, inner, some = place_of(j, n)
-            mixed = mix.total(h, inner)
-            change = states + gate[...] * mixed - target
-            diff[some, :] = change
-            own_up[h, inner, :] = (gate[...] * change).astype(BF)
-            both = change * mixed
-            gate_rows[...] += both[:8] + both[8:]
+        def tiles(cols):
+            rate = gate[:, cols]
+            both = zip(pieces(hidden, j, cols), pieces(teacher, j, cols))
+            for n, (states, target) in enumerate(both):
+                h, inner, some = place_of(j, n)
+                mixed = mix.total(h, inner, cols)
+                change = states + rate * mixed - target
+                diff[some, cols] = change
+                own_up[h, inner, cols] = (rate * change).astype(BF)
+                product = change * mixed
+                gate_rows[:, cols] += product[:8] + product[8:]
+
+        tile_loop(tiles)
 
     each_rows(compare)
     leaving = [
@@ -1000,12 +1005,17 @@
     shift_rows[...] = jnp.zeros_like(shift_rows)
 
     def add_up(j):
-        for n, states in enumerate(pieces(hidden, j)):
-            h, inner, _ = place_of(j, n)
-            dmod = back.total(h, inner)
-            both = dmod * (states * row_factor(states))
-            scale_rows[...] += both[:8] + both[8:]
-            shift_rows[...] += dmod[:8] + dmod[8:]
+        rates = [row_factor(states) for states in pieces(hidden, j)]
+
+        def tiles(cols):
+            for n, states in enumerate(pieces(hidden, j, cols)):
+                h, inner, _ = place_of(j, n)
+                dmod = back.total(h, inner, cols)
+                both = dmod * (states * rates[n])
+                scale_rows[:, cols] += both[:8] + both[8:]
+                shift_rows[:, cols] += dmod[:8] + dmod[8:]
+
+        tile_loop(tiles)
 
     def close(j):
         done = []

time: 260 us -> 260 us (level)
  no operation moved by 1% of the time
where the time goes in v7:
time: 260 us; the launch traced here: 259 us
  Pallas kernels  259 us (100%)
    pallas_call x1, Pallas kernels, front(): pl.pallas_call(front_kernel, out_shape=[kept, kept, jax.ShapeDtypeStruct(...  160 us
    pallas_call x1, Pallas kernels, rear(): pl.pallas_call(rear_kernel, out_shape=[jax.ShapeDtypeStruct((2, HALF, WID...  96.4 us

profile of v7, /device:TPU:1, one launch (start us, length us, event | category | flops | bytes accessed | tf_op | source)
XLA Modules:
  0.0 259.2 jit_solution(8348744350812092142)
XLA Ops:
  0.6 159.7 %front.1 = (bf16[2,4,2,64,3072]{4,3,2,1,0:T(8,128)(2,1)}, bf16[2,4,2,64,3072]{4,3,2,1,0:T(8,128)(2,1)}, bf16[4,16,16,1152]{3,2,1,0:T(8,128)(2,1)}, f32[2,4,128,1...) custom-call(bf16[2,64,3072]{2,1,0:T(8,128)(2,1)} %hidden_hbm.1, ...), custom_call_target="tpu_custom_call" | custom-call | flops 12079595520 | bytes 50000000 | tf_op jit(solution)/shard_map/front/pallas_call | solution.py:867
  160.3 96.4 %rear.1 = (bf16[2,64,3072]{2,1,0:T(8,128)(2,1)}, bf16[3,192,384]{2,1,0:T(8,128)(2,1)}, bf16[192,384]{1,0:T(8,128)(2,1)}, f32[8,3072]{1,0:T(8,128)}) custom-call(f32[8,3072]{1,0:T(8,128)} %get-tuple-element.24.gate_rows, f32[1,3072]{1,0:T(1,128)} %bitcast.11, bf16[4,16,16,1152]{3,2,1,0:T(8,128)(2,1)} %get-tuple-element.25.qkv, ...), custom_call_target="tpu_custom_call" | custom-call | flops 16911433728 | bytes 50000000 | tf_op jit(solution)/shard_map/rear/pallas_call | solution.py:1045
  256.8 2.4 hand_over.1
